TPU v7x, 512 devices: a whole 4x4x16 slice. The times are simulated.
512 devices in a mesh: expert: 8 (over x, y_hi), etp: 64 (over z, y_lo, core).
Axes of the slice: x: 4, y: 4 (y_hi: 2, y_lo: 2; y = y_hi * 2 + y_lo), z: 16, core: 2. Of those that a mesh axis runs over, the one named last changes fastest.
Arguments:
- tokens: bfloat16 [1024, 3072], P('expert'), may hold values from -6 to 6
- routes: int32 [1024, 2], P('expert'), may hold values from 0 to 7, all different within a row; in each aligned block of 128 rows (0 to 127, 128 to 255, ...) at most 40 rows name the same one
- w_gate: bfloat16 [8, 3072, 8192], P('expert', None, 'etp'), may hold values from -0.3125 to 0.3125
- w_up: bfloat16 [8, 3072, 8192], P('expert', None, 'etp'), may hold values from -0.3125 to 0.3125
- d_hidden: bfloat16 [1024, 2, 8192], P('expert', None, 'etp'), may hold values from -6 to 6
Outputs:
- d_tokens: bfloat16 [1024, 3072], P('expert', 'etp')
- update_gate: bfloat16 [8, 3072, 8192], P('expert', None, 'etp')
- update_up: bfloat16 [8, 3072, 8192], P('expert', None, 'etp')
Inputs may be any that keep to these rules, and one draw needn't show every extreme that they name: `routes`: in each aligned block of 128 rows (the tokens of one index of expert) a row names two different experts, no expert is named by more than 40 rows, a bound that some block reaches.
All inputs are finite; a program needn't handle non-finite values.
Results may differ from a plain program's by a relative error of at most 0.0055.
Values may be sent and summed in bfloat16 or wider, within the bound.
A program may use at most 64 MiB of HBM per device.

v0:
```python
import jax
import jax.numpy as jnp
from jax import lax
from jax.sharding import PartitionSpec as P

NS_STEPS = 3
BLK = 128


ns_first = 3.4445
ns_second = -4.775
ns_third = 2.0315


def routing(route_block, experts, capacity):
    choices_flat = route_block.reshape(-1)
    chosen = (choices_flat[:, None] == jnp.arange(experts, dtype=jnp.int32)[None, :]).astype(
        jnp.int32
    )
    earlier = jnp.cumsum(chosen, axis=0) - chosen
    position = jnp.sum(earlier * chosen, axis=1)
    destination = choices_flat * capacity + position
    placing = (
        jnp.arange(experts * capacity, dtype=jnp.int32)[:, None] == destination[None, :]
    ).astype(jnp.float32)
    return placing


def orthogonalize(gradient):
    squares = jnp.sum(gradient * gradient)
    current = gradient * lax.rsqrt(squares + 1e-06)
    for iteration in range(NS_STEPS):
        gram_matrix = lax.dot_general(
            current,
            current,
            (((0,), (0,)), ((), ())),
            precision=lax.Precision.HIGHEST,
            preferred_element_type=jnp.float32,
        )
        mixing = ns_second * gram_matrix + ns_third * jnp.dot(
            gram_matrix, gram_matrix, precision=lax.Precision.HIGHEST
        )
        current = ns_first * current + jnp.dot(current, mixing, precision=lax.Precision.HIGHEST)
    return current.astype(jnp.bfloat16)


def blockwise(gradient):
    model_width, columns = gradient.shape
    blocks = gradient.reshape(model_width, columns // BLK, BLK).transpose(1, 0, 2)
    done = lax.map(orthogonalize, blocks)
    return done.transpose(1, 0, 2).reshape(model_width, columns)


def body(tokens, routes, w_gate, w_up, d_hidden):
    experts = lax.axis_size("expert")
    shards = lax.axis_size("etp")
    tok_count, model_width = tokens.shape
    hidden_units = w_gate.shape[2]
    capacity = min(tok_count, 5 * tok_count // (2 * experts))
    narrow = model_width // shards
    placing = routing(routes, experts, capacity)
    per_token = placing.reshape(experts * capacity, tok_count, 2).sum(axis=2)
    rows_out = jnp.dot(
        per_token.astype(jnp.bfloat16), tokens, preferred_element_type=jnp.float32
    ).astype(jnp.bfloat16)
    rows_out = rows_out.reshape(experts, capacity, model_width)
    cotangent_out = jnp.dot(
        placing.astype(jnp.bfloat16),
        d_hidden.reshape(2 * tok_count, hidden_units),
        preferred_element_type=jnp.float32,
    ).astype(jnp.bfloat16)
    cotangent_out = cotangent_out.reshape(experts, capacity, hidden_units)
    got_rows, got_cotangent = (
        lax.all_to_all(rows_out, "expert", split_axis=0, concat_axis=0, tiled=True),
        lax.all_to_all(cotangent_out, "expert", split_axis=0, concat_axis=0, tiled=True),
    )
    slot_rows = got_rows.reshape(experts * capacity, model_width)
    slot_cotangent = got_cotangent.reshape(experts * capacity, hidden_units)
    gate_weight = w_gate[0]
    up_weight = w_up[0]
    gate_act = jnp.dot(slot_rows, gate_weight, preferred_element_type=jnp.float32)
    up_act = jnp.dot(slot_rows, up_weight, preferred_element_type=jnp.float32)
    sigmoid_gate = jax.nn.sigmoid(gate_act)
    d_up = (slot_cotangent * gate_act * sigmoid_gate).astype(jnp.bfloat16)
    d_gate = (
        slot_cotangent * up_act * sigmoid_gate * (1.0 + gate_act * (1.0 - sigmoid_gate))
    ).astype(jnp.bfloat16)
    contract_units = (((1,), (1,)), ((), ()))
    back_rows = lax.dot_general(
        d_gate, gate_weight, contract_units, preferred_element_type=jnp.float32
    )
    back_rows = back_rows + lax.dot_general(
        d_up, up_weight, contract_units, preferred_element_type=jnp.float32
    )
    contract_rows = (((0,), (0,)), ((), ()))
    shares = lax.psum_scatter(back_rows, "etp", scatter_dimension=1, tiled=True)
    returned = lax.all_to_all(
        shares.reshape(experts, capacity, narrow), "expert", split_axis=0, concat_axis=0, tiled=True
    )
    d_tokens = lax.dot_general(
        per_token,
        returned.reshape(experts * capacity, narrow),
        contract_rows,
        precision=lax.Precision.HIGHEST,
        preferred_element_type=jnp.float32,
    )
    grad_gate = lax.dot_general(
        slot_rows, d_gate, contract_rows, preferred_element_type=jnp.float32
    )
    grad_up = lax.dot_general(slot_rows, d_up, contract_rows, preferred_element_type=jnp.float32)
    update_gate = blockwise(grad_gate)[None]
    update_up = blockwise(grad_up)[None]
    return (d_tokens.astype(jnp.bfloat16), update_gate, update_up)


def solution(mesh):
    in_specs = (
        P("expert", None),
        P("expert", None),
        P("expert", None, "etp"),
        P("expert", None, "etp"),
        P("expert", None, "etp"),
    )
    out_specs = (P("expert", "etp"), P("expert", None, "etp"), P("expert", None, "etp"))
    return jax.shard_map(body, mesh=mesh, in_specs=in_specs, out_specs=out_specs, check_vma=False)
```

profile of v0, /device:TPU:1, one launch (start us, length us, event | category | flops | bytes accessed | tf_op | source)
XLA Modules:
  0.0 316.8 jit_solution(11507911879526677713)
XLA Ops:
  9.3 1.7 convolution_convert_fusion.1
  11.0 7.5 %all-to-all-start = ((bf16[8,40,128]{2,1,0:T(8,128)(2,1)}), bf16[8,40,128]{2,1,0:T(8,128)(2,1)S(1)}, u32[]{:S(2)}, u32[]{:S(2)}) async-start(bf16[8,40,128]{2,1,0:T(8,128)(2,1)} %bitcast.3), calls=%async_computation | async-start | bytes 163840 | tf_op jit(solution)/shard_map/all_to_all | solution.py:75
  19.4 3.1 convolution_convert_fusion
  22.5 2.6 all-to-all-done
  25.1 27.3 %all_to_all.15 = bf16[8,40,3072]{2,1,0:T(8,128)(2,1)S(1)} all-to-all(bf16[8,40,3072]{2,1,0:T(8,128)(2,1)} %bitcast.79), channel_id=1, replica_groups=mesh['expert'=8,'etp'=64] {'expert'}, dimensions={0} | all-to-all | bytes 3932160 | tf_op jit(solution)/shard_map/all_to_all | solution.py:74
  55.0 2.9 convolution_add_fusion
  57.9 2.6 multiply_reduce_fusion
  61.2 2.7 multiply_reduce_fusion.1
  64.7 4.7 %fusion.4 = f32[128,128]{1,0:T(8,128)S(1)} fusion(f32[3072,128]{1,0:T(8,128)} %get-tuple-element.26, f32[]{:T(128)S(6)} %rsqrt.9), kind=kOutput, calls=%fused_computation.14 | convolution fusion | flops 604372992 | bytes 1638404 | tf_op jit(solution)/shard_map/while/body/eval_jaxpr/dot_general | solution.py:33
  69.6 1.4 convolution_add_fusion.3
  71.0 2.7 fusion.38
  74.0 1.6 convolution_add_fusion.2
  75.6 2.7 fusion.39
  78.6 2.3 fusion.2
  80.9 2.7 fusion.7
  83.8 1.4 convolution_add_fusion.6
  85.2 2.9 fusion.36
  88.4 1.4 convolution_add_fusion.5
  89.8 2.6 fusion.37
  92.7 200.5 %reduce-scatter.2.cloned.1.call-done = f32[320,48]{0,1:T(8,128)} async-done(((f32[320,3072]{0,1:T(8,128)}), f32[320,48]{0,1:T(8,128)}) %reduce-scatter.2.cloned.1.call-update) | async-done | bytes 61456 | tf_op jit(solution)/shard_map/reduce_scatter | solution.py:96
  295.0 5.9 %all-to-all-start.2 = ((f32[8,1,1920]{2,1,0:T(1,128)}), f32[8,1,1920]{2,1,0:T(1,128)S(1)}, u32[]{:S(2)}, u32[]{:S(2)}) async-start(f32[8,1,1920]{2,1,0:T(1,128)} %reshape.76), calls=%async_computation.3 | async-start | bytes 122880 | tf_op jit(solution)/shard_map/all_to_all | solution.py:97
  300.9 2.3 fusion.3
  303.1 4.3 %all-to-all-done.2 = f32[8,1,1920]{2,1,0:T(1,128)S(1)} async-done(((f32[8,1,1920]{2,1,0:T(1,128)}), f32[8,1,1920]{2,1,0:T(1,128)S(1)}, u32[]{:S(2)}, u32[]{:S(2)}) %all-to-all-start.2) | async-done | bytes 61472 | tf_op jit(solution)/shard_map/all_to_all | solution.py:97
  308.9 1.0 convolution_convert_fusion.2
  (38 shorter events, 10.1 us)
Async XLA Ops:
  7.2 45.2 %copy-start = (bf16[1,3072,128]{2,1,0:T(8,128)(2,1)S(1)}, bf16[1,3072,128]{2,1,0:T(8,128)(2,1)}, u32[]{:S(2)}) copy-start(bf16[1,3072,128]{2,1,0:T(8,128)(2,1)} %param.7) | copy-start | bytes 2359300
  11.0 14.1 %all-to-all-start = ((bf16[8,40,128]{2,1,0:T(8,128)(2,1)}), bf16[8,40,128]{2,1,0:T(8,128)(2,1)S(1)}, u32[]{:S(2)}, u32[]{:S(2)}) async-start(bf16[8,40,128]{2,1,0:T(8,128)(2,1)} %bitcast.3), calls=%async_computation | async-start | bytes 163840 | tf_op jit(solution)/shard_map/all_to_all | solution.py:75
  18.4 274.7 %reduce-scatter.2.cloned.1.call-start = ((), (), s32[]{:S(2)}) async-start(), calls=%async_computation.4 | async-start | bytes 4792320 | tf_op jit(solution)/shard_map/reduce_scatter | solution.py:96
  52.4 1.1 copy-start.3
  63.9 5.7 %copy-start.2 = (f32[3072,128]{1,0:T(8,128)S(1)}, f32[3072,128]{1,0:T(8,128)}, u32[]{:S(2)}) copy-start(f32[3072,128]{1,0:T(8,128)} %get-tuple-element.26) | copy-start | bytes 4718596
  78.3 2.5 copy-start.1
  295.0 12.5 %all-to-all-start.2 = ((f32[8,1,1920]{2,1,0:T(1,128)}), f32[8,1,1920]{2,1,0:T(1,128)S(1)}, u32[]{:S(2)}, u32[]{:S(2)}) async-start(f32[8,1,1920]{2,1,0:T(1,128)} %reshape.76), calls=%async_computation.3 | async-start | bytes 122880 | tf_op jit(solution)/shard_map/all_to_all | solution.py:97
Sparse Core Ops, SparseCore 0:
  58.0 235.1 reduce-scatter.1
where the time goes:
time: 321 us; the launch traced here: 317 us
  waiting for transfers between devices  207 us (64%)
  matrix products  46.2 us (14%)
  blocking collectives  27.3 us (9%)
  between operations  15.7 us (5%)
  starting transfers between devices  13.4 us (4%)
  local copies, waits for them, and re-layouts  4.41 us (1%)
    reduce_scatter x1, waiting for transfers between devices, body(): shares = lax.psum_scatter(back_rows, 'etp', scatter_dimension=1, tiled=True)  201 us
    all_to_all x1, blocking collectives, body(): lax.all_to_all(rows_out, 'expert', split_axis=0, concat_axis=0, tiled=True)  27.3 us
    dot_general x6, matrix products, orthogonalize(): lax.dot_general(current, current, (((0,), (0,)), ((), ())), precision=lax...  18.4 us
    dot_general x6, matrix products, orthogonalize(): jnp.dot(current, mixing, precision=lax.Precision.HIGHEST)  10.5 us
    all_to_all x1, starting transfers between devices, body(): lax.all_to_all(cotangent_out, 'expert', split_axis=0, concat_axis=0, tile...  7.48 us
  transfers between devices with their start and end apart: 3, of which 3 were waited for; matrix products, arithmetic and copies ran while one was open for 12% of the time, Pallas kernels for 0%

commit v1 on v0

v1 whole, which is shorter than its diff:
```python
import functools

import jax
import jax.numpy as jnp
from jax import lax
from jax.experimental import pallas as pl
from jax.experimental.pallas import tpu as pltpu
from jax.sharding import PartitionSpec as P

EXPERTS = 8
ZS = 16
BLK = 128
CAP = 40
SLOTS = EXPERTS * CAP
NSUB = 2
STARTS = (0, 128)
SIZES = (128, 112)

NS_FIRST = 3.4445
NS_SECOND = -4.775
NS_THIRD = 2.0315

MESH = pl.DeviceIdType.MESH
F32 = jnp.float32
BF16 = jnp.bfloat16


def dot(a, b):
    return jnp.dot(a, b, preferred_element_type=F32)


def dot_nt(a, b):
    return lax.dot_general(a, b, (((1,), (1,)), ((), ())), preferred_element_type=F32)


def dot_exact(a, b):
    return jnp.dot(a, b, precision=lax.Precision.HIGHEST, preferred_element_type=F32)


def kernel(
    tokens_ref,
    routes_ref,
    w_gate_ref,
    w_up_ref,
    dh_ref,
    d_tokens_ref,
    update_gate_ref,
    update_up_ref,
    tok,
    wcat,
    rows_out,
    land,
    cot_out,
    cot_land,
    srows,
    a_hi,
    a_lo,
    gram,
    mix,
    bt_own,
    bt_send,
    bt_recv,
    ring_out,
    ring_in,
    ret_out,
    ret_in,
    pmat,
    in_sem,
    s1_send,
    s1_recv,
    cot_send,
    cot_recv,
    z_send,
    z_recv,
    c0_send,
    c0_recv,
    c2_send,
    c2_recv,
    x_send,
    x_recv,
    ring_send,
    ring_recv,
    ret_send,
    ret_recv,
):
    expert = lax.axis_index("expert")
    p = lax.axis_index("etp")
    z = p // 4
    y = (p // 2) % 2
    core = p % 2
    width = tok.shape[1]
    half = width // 2

    def peer(o):
        return (expert + o) % EXPERTS

    core_mate = z * 4 + y * 2 + (1 - core)
    z_up = (p + 4) % (4 * ZS)
    z_down = (p + 4 * ZS - 4) % (4 * ZS)
    z_to = (p + 4 * ZS + 4 - 8 * core) % (4 * ZS)
    y_mate = z * 4 + (1 - y) * 2 + core

    own_q = 2 * (z % 2) + core
    mate_q = 2 * (z % 2) + (1 - core)
    zown_q = 2 * (1 - z % 2) + core
    zmate_q = 2 * (1 - z % 2) + (1 - core)
    quarters = (own_q, mate_q, zown_q, zmate_q)

    tok_copy = pltpu.make_async_copy(
        tokens_ref.at[:, pl.ds(pl.multiple_of(own_q * width, 128), width)], tok, in_sem.at[0]
    )
    wg_copy = pltpu.make_async_copy(w_gate_ref.at[0], wcat.at[:, pl.ds(0, BLK)], in_sem.at[1])
    wu_copy = pltpu.make_async_copy(w_up_ref.at[0], wcat.at[:, pl.ds(BLK, BLK)], in_sem.at[2])
    tok_copy.start()
    wg_copy.start()
    wu_copy.start()

    barrier = pltpu.get_barrier_semaphore()

    def greet(e, d):
        pl.semaphore_signal(
            barrier, inc=1, device_id={"expert": e, "etp": d}, device_id_type=MESH
        )

    greet(expert, core_mate)
    greet(expert, z_up)
    greet(expert, z_down)
    for o in range(1, EXPERTS):
        greet(peer(o), p)
    for o in range(EXPERTS):
        greet(peer(o), y_mate)

    lane = lax.broadcasted_iota(jnp.int32, (128, 128), 1)
    row = lax.broadcasted_iota(jnp.int32, (128, 128), 0)
    names_0 = jnp.where(lane == routes_ref[:, 0:1], 1.0, 0.0).T
    names_1 = jnp.where(lane == routes_ref[:, 1:2], 1.0, 0.0).T
    names = names_0 + names_1
    before = jnp.where(row < lane, 1.0, 0.0).astype(BF16)
    position = dot(names.astype(BF16), before)
    position = jnp.where(names > 0.5, position, -1.0)
    rowf = row.astype(F32)
    tall, first, second = [], [], []
    for e in range(EXPERTS):
        place = jnp.where(rowf == position[e : e + 1, :], 1.0, 0.0)
        pmat[e] = place.astype(BF16)
        place = place[:CAP]
        tall.append(place)
        first.append(place * names_0[e : e + 1, :])
        second.append(place * names_1[e : e + 1, :])
    tall = jnp.concatenate(tall, axis=0).astype(BF16)
    first = jnp.concatenate(first, axis=0).astype(BF16)
    second = jnp.concatenate(second, axis=0).astype(BF16)
    token_of = lax.broadcasted_iota(jnp.int32, (128, 256), 0)
    choice = lax.broadcasted_iota(jnp.int32, (128, 256), 1)
    even = jnp.where(choice == 2 * token_of, 1.0, 0.0).astype(BF16)
    odd = jnp.where(choice == 2 * token_of + 1, 1.0, 0.0).astype(BF16)
    placing = (dot(first, even) + dot(second, odd)).astype(BF16)
    cot = dot(placing, dh_ref[...])
    for e in range(EXPERTS):
        padded = jnp.concatenate(
            [cot[CAP * e : CAP * e + CAP], jnp.zeros((8, 128), F32)], axis=0
        )
        cot_out[e] = padded.astype(BF16)
    tok_copy.wait()
    placed = dot(tall, tok[...])
    for e in range(EXPERTS):
        rows = placed[CAP * e : CAP * e + CAP]
        rows_out[e] = jnp.concatenate([rows[:, :half], rows[:, half:]], axis=0).astype(BF16)

    pl.semaphore_wait(barrier, 3 + (EXPERTS - 1) + EXPERTS)

    sends = []

    def remote(src, dst, send_sem, recv_sem, e, d):
        copy = pltpu.make_async_remote_copy(
            src_ref=src,
            dst_ref=dst,
            send_sem=send_sem,
            recv_sem=recv_sem,
            device_id={"expert": e, "etp": d},
            device_id_type=MESH,
        )
        sends.append(copy)
        return copy

    stage1, cots, zfwd, c0fwd, c2fwd = {}, {}, {}, {}, {}
    for o in range(1, EXPERTS):
        stage1[o] = remote(
            rows_out.at[peer(o)], land.at[0, o], s1_send.at[o], s1_recv.at[o], peer(o), p
        )
        stage1[o].start()
    for o in range(1, EXPERTS):
        cots[o] = remote(
            cot_out.at[peer(o)], cot_land.at[o], cot_send.at[o], cot_recv.at[o], peer(o), p
        )
        cots[o].start()
    land[0, 0] = rows_out[expert]
    cot_land[0] = cot_out[expert]

    for o in range(EXPERTS):
        if o > 0:
            stage1[o].wait_recv()
        zfwd[o] = remote(
            land.at[0, o], land.at[2, o], z_send.at[o], z_recv.at[o], expert, z_to
        )
        zfwd[o].start()
        c0fwd[o] = remote(
            land.at[0, o], land.at[1, o], c0_send.at[o], c0_recv.at[o], expert, core_mate
        )
        c0fwd[o].start()

    def compact(r):
        for j in range(EXPERTS // 2):
            one = land[r, 2 * j].astype(F32)
            two = land[r, 2 * j + 1].astype(F32)
            left = jnp.concatenate([one[:CAP], two[:CAP]], axis=0)
            right = jnp.concatenate([one[CAP:], two[CAP:]], axis=0)
            srows[r, pl.ds(2 * CAP * j, 2 * CAP), pl.ds(0, half)] = left.astype(BF16)
            srows[r, pl.ds(2 * CAP * j, 2 * CAP), pl.ds(half, half)] = right.astype(BF16)

    def forward(r):
        at = pl.multiple_of(quarters[r] * width, 128)
        return dot(srows[r], wcat[pl.ds(at, width), :])

    wg_copy.wait()
    wu_copy.wait()
    compact(0)
    acts = forward(0)
    for o in range(EXPERTS):
        zfwd[o].wait_recv()
        c2fwd[o] = remote(
            land.at[2, o], land.at[3, o], c2_send.at[o], c2_recv.at[o], expert, core_mate
        )
        c2fwd[o].start()
    for o in range(EXPERTS):
        c0fwd[o].wait_recv()
    compact(1)
    acts = acts + forward(1)
    compact(2)
    acts = acts + forward(2)
    for o in range(EXPERTS):
        c2fwd[o].wait_recv()
    compact(3)
    acts = acts + forward(3)

    for o in range(1, EXPERTS):
        cots[o].wait_recv()
    cotangent = jnp.concatenate(
        [cot_land[o].astype(F32)[:CAP] for o in range(EXPERTS)], axis=0
    )
    gate_act, up_act = acts[:, :BLK], acts[:, BLK:]
    sig = jax.nn.sigmoid(gate_act)
    d_up = cotangent * gate_act * sig
    d_gate = cotangent * up_act * sig * (1.0 + gate_act * (1.0 - sig))
    d_both = jnp.concatenate([d_gate, d_up], axis=1)
    d_both = jnp.concatenate([d_both, jnp.zeros((384 - SLOTS, 2 * BLK), F32)], axis=0)
    d_t = d_both.T.astype(BF16)

    gz = z // 4
    groups = [(gz + 2) % 4, (gz + 3) % 4, (gz + 1) % 4, gz]
    lower = lax.broadcasted_iota(jnp.int32, (48, 128), 1) < 64
    swaps = []
    first_core = core == 0
    for g in range(4):
        at = pl.multiple_of(groups[g] * width, 128)
        back = dot(wcat[pl.ds(at, width), :], d_t)
        for i in range(4):
            part = back[192 * i : 192 * i + 192]
            parts = [part[48 * k : 48 * k + 48] for k in range(4)]
            for mine in (True, False):
                pick = []
                for k in range(2):
                    a, b = parts[2 * k], parts[2 * k + 1]
                    if not mine:
                        a, b = b, a
                    pick.append(jnp.where(first_core, a, b))
                folded = pick[0][:, 256:] + pltpu.roll(pick[1][:, 256:], 64, 1)
                whole = jnp.concatenate(
                    [pick[0][:, :128], pick[1][:, :128], pick[0][:, 128:256], pick[1][:, 128:256], folded],
                    axis=0,
                )
                if mine:
                    bt_own[groups[g] * 4 + i] = whole
                else:
                    bt_send[groups[g] * 4 + i] = whole.astype(BF16)
        swap = remote(
            bt_send.at[pl.ds(groups[g] * 4, 4)],
            bt_recv.at[pl.ds(groups[g] * 4, 4)],
            x_send.at[g],
            x_recv.at[g],
            expert,
            core_mate,
        )
        swap.start()
        swaps.append(swap)

    def grad_piece(r):
        grad = dot(d_t[:, :SLOTS], srows[r])
        hi = grad.astype(BF16)
        lo = (grad - hi.astype(F32)).astype(BF16)
        a_hi[r] = hi
        a_lo[r] = lo

    def gram_piece(r):
        hi, lo = a_hi[r], a_lo[r]
        if r == 0:
            gram[0] = dot_nt(hi, hi)
            gram[1] = dot_nt(hi, lo)
        else:
            gram[0] = gram[0] + dot_nt(hi, hi)
            gram[1] = gram[1] + dot_nt(hi, lo)

    wide_row = lax.broadcasted_iota(jnp.int32, (256, 256), 0)
    wide_lane = lax.broadcasted_iota(jnp.int32, (256, 256), 1)
    state = {}

    def ns_start():
        cross = gram[1]
        g = gram[0] + cross + cross.T
        g = jnp.where((wide_row < BLK) == (wide_lane < BLK), g, 0.0)
        diagonal = jnp.where(wide_row == wide_lane, g, 0.0)
        sum_gate = jnp.sum(diagonal[:BLK], keepdims=True)
        sum_up = jnp.sum(diagonal[BLK:], keepdims=True)
        scale = jnp.where(
            wide_row < BLK, lax.rsqrt(sum_gate + 1e-06), lax.rsqrt(sum_up + 1e-06)
        )
        state["scale"] = scale
        state["g"] = g * scale * scale

    def polynomial(g):
        square = dot_exact(g, g)
        return jnp.where(wide_row == wide_lane, NS_FIRST, 0.0) + NS_SECOND * g + NS_THIRD * square

    def ns_one():
        g = state["g"]
        poly = polynomial(g)
        state["m"] = poly
        state["g"] = dot_exact(dot_exact(g, poly), poly)

    def ns_two():
        g = state["g"]
        poly = polynomial(g)
        both = dot_exact(jnp.concatenate([state["m"], g], axis=0), poly)
        state["m"] = both[:256]
        state["g"] = dot_exact(both[256:], poly)

    def ns_three():
        m = dot_exact(state["m"], polynomial(state["g"])) * state["scale"]
        hi = m.astype(BF16)
        mix[0] = hi
        mix[1] = (m - hi.astype(F32)).astype(BF16)

    def update_piece(r):
        hi = a_hi[r]
        update = dot(mix[0], hi) + dot(mix[1], hi) + dot(mix[0], a_lo[r])
        update = update.T.astype(BF16)
        at = pl.multiple_of(quarters[r] * width, 128)
        update_gate_ref[0, pl.ds(at, width), :] = update[:, :BLK]
        update_up_ref[0, pl.ds(at, width), :] = update[:, BLK:]

    def both_pieces(r):
        grad_piece(r)
        gram_piece(r)

    tasks = [functools.partial(both_pieces, r) for r in range(4)]
    tasks += [ns_start, ns_one, ns_two, ns_three]
    tasks += [functools.partial(update_piece, r) for r in range(4)]
    plan = {0: 1, 1: 1, 2: 1, 3: 1, 4: 2, 5: 1, 6: 1, 7: 4}

    steps = ZS // 2
    up, down = {}, {}

    def send_chunk(which, slot, dst, previous, to):
        for i in range(NSUB):
            at = pl.ds(STARTS[i], SIZES[i])
            value = bt_own[dst, at] + bt_recv[dst, at].astype(F32)
            if previous is not None:
                previous[i].wait_recv()
                value = value + ring_in[slot - 1, at].astype(F32)
            ring_out[slot, at] = value.astype(BF16)
            copy = remote(
                ring_out.at[slot, at],
                ring_in.at[slot, at],
                ring_send.at[slot, i],
                ring_recv.at[slot, i],
                expert,
                to,
            )
            copy.start()
            which.setdefault(slot, []).append(copy)

    for s in range(steps):
        if s == 0:
            swaps[0].wait_recv()
            swaps[1].wait_recv()
        elif s == 1:
            swaps[2].wait_recv()
        elif s == 4:
            swaps[3].wait_recv()
        send_chunk(up, s, (z + steps - s) % ZS, up.get(s - 1), z_up)
        if s < steps - 1:
            slot = steps + s
            send_chunk(
                down, slot, (z + ZS - (steps - 1 - s)) % ZS, down.get(slot - 1), z_down
            )
        for _ in range(plan[s]):
            tasks.pop(0)()
    while tasks:
        tasks.pop(0)()
    pieces = []
    for i in range(NSUB):
        at = pl.ds(STARTS[i], SIZES[i])
        up[steps - 1][i].wait_recv()
        down[2 * steps - 2][i].wait_recv()
        pieces.append(
            bt_own[z, at]
            + bt_recv[z, at].astype(F32)
            + ring_in[steps - 1, at].astype(F32)
            + ring_in[2 * steps - 2, at].astype(F32)
        )
    total = jnp.concatenate(pieces, axis=0)
    folded = total[192:]
    tail = jnp.concatenate(
        [jnp.where(lower, folded, 0.0), jnp.where(lower, pltpu.roll(folded, 64, 1), 0.0)], axis=0
    )
    total = jnp.concatenate([total[:96], total[96:192], tail], axis=1).astype(BF16)
    slot_of = lax.broadcasted_iota(jnp.int32, (384, 128), 0)
    place_of = lax.broadcasted_iota(jnp.int32, (384, 128), 1)
    for o in range(EXPERTS):
        spread = jnp.where((slot_of == place_of + CAP * o) & (place_of < CAP), 1.0, 0.0)
        block = dot(total, spread.astype(BF16)).astype(BF16)
        ret_out[o, 0] = block[:48]
        ret_out[o, 1] = block[48:]

    returns = []
    for dy in range(2):
        to_y = (y + dy) % 2
        for o in range(EXPERTS):
            if o == 0 and dy == 0:
                continue
            copy = remote(
                ret_out.at[o, to_y],
                ret_in.at[o, dy],
                ret_send.at[o, dy],
                ret_recv.at[o, dy],
                (expert + EXPERTS - o) % EXPERTS,
                z * 4 + to_y * 2 + core,
            )
            copy.start()
            returns.append(copy)
    ret_in[0, 0] = ret_out[0, y]
    for copy in returns:
        copy.wait_recv()
    out = jnp.zeros((48, 128), F32)
    for o in range(EXPERTS):
        place = pmat[peer(o)]
        out = out + dot(ret_in[o, 0], place) + dot(ret_in[o, 1], place)
    out = jnp.concatenate([out, jnp.zeros((80, 128), F32)], axis=0).T
    d_tokens_ref[...] = out[:, :48].astype(BF16)
    for copy in sends:
        copy.wait_send()


def body(tokens, routes, w_gate, w_up, d_hidden):
    count, model_width = tokens.shape
    units = w_gate.shape[2]
    width = model_width // 4
    half = width // 2
    steps = ZS - 1
    dma = pltpu.SemaphoreType.DMA
    scratch = [
        pltpu.VMEM((count, width), BF16),
        pltpu.VMEM((model_width, 2 * units), BF16),
        pltpu.VMEM((EXPERTS, 2 * CAP, half), BF16),
        pltpu.VMEM((4, EXPERTS, 2 * CAP, half), BF16),
        pltpu.VMEM((EXPERTS, 48, units), BF16),
        pltpu.VMEM((EXPERTS, 48, units), BF16),
        pltpu.VMEM((4, SLOTS, width), BF16),
        pltpu.VMEM((4, 2 * units, width), BF16),
        pltpu.VMEM((4, 2 * units, width), BF16),
        pltpu.VMEM((2, 2 * units, 2 * units), F32),
        pltpu.VMEM((2, 2 * units, 2 * units), BF16),
        pltpu.VMEM((ZS, 240, 128), F32),
        pltpu.VMEM((ZS, 240, 128), BF16),
        pltpu.VMEM((ZS, 240, 128), BF16),
        pltpu.VMEM((steps, 240, 128), BF16),
        pltpu.VMEM((steps, 240, 128), BF16),
        pltpu.VMEM((EXPERTS, 2, 48, 128), BF16),
        pltpu.VMEM((EXPERTS, 2, 48, 128), BF16),
        pltpu.VMEM((EXPERTS, 128, 128), BF16),
        dma((3,)),
    ]
    for shape in ((EXPERTS,), (EXPERTS,), (EXPERTS,), (EXPERTS,), (EXPERTS,), (4,), (steps, NSUB), (EXPERTS, 2)):
        scratch += [dma(shape), dma(shape)]
    vmem = pl.BlockSpec(memory_space=pltpu.VMEM)
    anywhere = pl.BlockSpec(memory_space=pl.ANY)
    return pl.pallas_call(
        kernel,
        out_shape=(
            jax.ShapeDtypeStruct((count, 48), BF16),
            jax.ShapeDtypeStruct(w_gate.shape, BF16),
            jax.ShapeDtypeStruct(w_up.shape, BF16),
        ),
        in_specs=[anywhere, vmem, anywhere, anywhere, vmem],
        out_specs=(vmem, vmem, vmem),
        scratch_shapes=scratch,
        compiler_params=pltpu.CompilerParams(
            collective_id=0, has_side_effects=True, vmem_limit_bytes=56 * 1024 * 1024
        ),
    )(tokens, routes, w_gate, w_up, d_hidden.reshape(2 * count, units))


def solution(mesh):
    in_specs = (
        P("expert", None),
        P("expert", None),
        P("expert", None, "etp"),
        P("expert", None, "etp"),
        P("expert", None, "etp"),
    )
    out_specs = (P("expert", "etp"), P("expert", None, "etp"), P("expert", None, "etp"))
    return jax.shard_map(body, mesh=mesh, in_specs=in_specs, out_specs=out_specs, check_vma=False)
```

time: 321 us -> 77.4 us (0.24)
  the two profiles are of different devices: /device:TPU:1 before, /device:TPU:32 now
where the time goes in v1:
time: 77.4 us; the launch traced here: 77.1 us
  Pallas kernels  70.5 us (91%)
  local copies, waits for them, and re-layouts  5.87 us (8%)
    pallas_call x1, Pallas kernels, body(): pl.pallas_call(kernel, out_shape=(jax.ShapeDtypeStruct((count, 48), BF16)...  70.5 us
    unnamed x7, local copies, waits for them, and re-layouts  4.43 us

profile of v1, /device:TPU:32, one launch (start us, length us, event | category | flops | bytes accessed | tf_op | source)
XLA Modules:
  0.0 77.1 jit_solution(1133731275838548467)
XLA Ops:
  0.6 0.0 copy-start.1
  0.6 0.7 copy-done.1
  1.3 0.7 copy.8.routes_ref
  2.1 70.5 %shard_map.76 = (bf16[128,48]{1,0:T(8,128)(2,1)}, bf16[1,3072,128]{2,1,0:T(8,128)(2,1)}, bf16[1,3072,128]{2,1,0:T(8,128)(2,1)}) custom-call(bf16[128,3072]{1,0:T(8,128)(2,1)} %tokens_ref.1, s32[128,2]{1,0:T(8,128)} %copy.8.routes_ref, bf16[1,3072,128]{2,1,0:T(8,128)(2,1)} %w_gate_ref.1, bf16[1,3072,128]{2,1,0:T(8,128)(2,1)} %w_up_ref.1, bf16[256,128]{1,0:T(8,128)(2,1)} %bitcast.1), custom_call_target="tpu_custom_call" | custom-call | tf_op jit(solution)/shard_map/pallas_call | solution.py:497
  72.6 1.4 %copy.9 = bf16[128,48]{0,1:T(8,128)(2,1)} copy(bf16[128,48]{1,0:T(8,128)(2,1)} %get-tuple-element.3) | data formatting | bytes 24576 | tf_op jit(solution)/shard_map/pallas_call | solution.py:497
  74.0 0.0 copy-start
  74.0 2.1 %copy.12 = bf16[1,3072,128]{2,1,0:T(8,128)(2,1)} copy(bf16[1,3072,128]{2,1,0:T(8,128)(2,1)} %get-tuple-element.10) | data formatting | bytes 1572864
  76.2 0.0 copy-done
  76.2 0.9 %copy.13 = bf16[1,3072,128]{2,1,0:T(8,128)(2,1)} copy(bf16[1,3072,128]{2,1,0:T(8,128)(2,1)S(1)} %copy-done) | data formatting | bytes 1572864
Async XLA Ops:
  0.6 0.7 copy-start.1
  74.0 2.1 %copy-start = (bf16[1,3072,128]{2,1,0:T(8,128)(2,1)S(1)}, bf16[1,3072,128]{2,1,0:T(8,128)(2,1)}, u32[]{:S(2)}) copy-start(bf16[1,3072,128]{2,1,0:T(8,128)(2,1)} %get-tuple-element.11) | copy-start | bytes 2359300

commit v2 on v1

v2 whole, which is shorter than its diff:
```python
import functools

import jax
import jax.numpy as jnp
from jax import lax
from jax.experimental import pallas as pl
from jax.experimental.pallas import tpu as pltpu
from jax.sharding import PartitionSpec as P

EXPERTS = 8
ZS = 16
BLK = 128
CAP = 40
SLOTS = EXPERTS * CAP
PARTS = 3
FAR_FIRST = (5, 3, 4, 7, 1, 6, 2)
ORDER = (8, 7, 9, 6, 10, 5, 11, 12, 4, 3, 13, 2, 14, 1, 15, 0)
WORK = (8, 3, 1)

NS_FIRST = 3.4445
NS_SECOND = -4.775
NS_THIRD = 2.0315

MESH = pl.DeviceIdType.MESH
F32 = jnp.float32
BF16 = jnp.bfloat16


def dot(a, b):
    return jnp.dot(a, b, preferred_element_type=F32)


def dot_nt(a, b):
    return lax.dot_general(a, b, (((1,), (1,)), ((), ())), preferred_element_type=F32)


def dot_exact(a, b):
    return jnp.dot(a, b, precision=lax.Precision.HIGHEST, preferred_element_type=F32)


def kernel(
    tokens_ref,
    routes_ref,
    w_gate_ref,
    w_up_ref,
    dh_ref,
    d_tokens_ref,
    update_gate_ref,
    update_up_ref,
    routes,
    tok,
    dh,
    updates,
    wcat,
    rows_out,
    land,
    cot_out,
    cot_land,
    srows,
    a_hi,
    a_lo,
    gram,
    mix,
    swap_out,
    swap_in,
    first_out,
    first_in,
    later_out,
    later_in,
    zx_out,
    zx_in,
    pmat,
    in_sem,
    out_sem,
    s1_send,
    s1_recv,
    cot_send,
    cot_recv,
    z_send,
    z_recv,
    c0_send,
    c0_recv,
    c2_send,
    c2_recv,
    swap_send,
    swap_recv,
    a2a_send,
    a2a_recv,
    zx_send,
    zx_recv,
):
    expert = lax.axis_index("expert")
    p = lax.axis_index("etp")
    z = p // 4
    y = (p // 2) % 2
    core = p % 2
    width = tok.shape[1]
    half = width // 2

    def peer(o):
        return (expert + o) % EXPERTS

    def back_peer(o):
        return (expert + EXPERTS - o) % EXPERTS

    core_mate = z * 4 + y * 2 + (1 - core)
    z_to = (p + 4 * ZS + 4 - 8 * core) % (4 * ZS)
    y_mate = z * 4 + (1 - y) * 2 + core

    def near(e):
        cross = (expert + e) % 2
        return z * 4 + ((y + cross) % 2) * 2 + core

    own_q = 2 * (z % 2) + core
    mate_q = 2 * (z % 2) + (1 - core)
    zown_q = 2 * (1 - z % 2) + core
    zmate_q = 2 * (1 - z % 2) + (1 - core)
    quarters = (own_q, mate_q, zown_q, zmate_q)

    tok_copy = pltpu.make_async_copy(
        tokens_ref.at[:, pl.ds(pl.multiple_of(own_q * width, 128), width)], tok, in_sem.at[0]
    )
    wg_copy = pltpu.make_async_copy(w_gate_ref.at[0], wcat.at[:, pl.ds(0, BLK)], in_sem.at[1])
    wu_copy = pltpu.make_async_copy(w_up_ref.at[0], wcat.at[:, pl.ds(BLK, BLK)], in_sem.at[2])
    dh_copy = pltpu.make_async_copy(dh_ref, dh, in_sem.at[3])
    routes_copy = pltpu.make_async_copy(routes_ref, routes, in_sem.at[4])
    routes_copy.start()
    tok_copy.start()
    dh_copy.start()
    wg_copy.start()
    wu_copy.start()

    barrier = pltpu.get_barrier_semaphore()

    def greet(e, d):
        pl.semaphore_signal(
            barrier, inc=1, device_id={"expert": e, "etp": d}, device_id_type=MESH
        )

    for o in range(1, EXPERTS):
        greet(peer(o), p)
    for o in range(EXPERTS):
        greet(peer(o), y_mate)
    greet(expert, core_mate)
    for dz in range(1, ZS):
        greet(expert, (p + 4 * dz) % (4 * ZS))

    lane = lax.broadcasted_iota(jnp.int32, (128, 128), 1)
    row = lax.broadcasted_iota(jnp.int32, (128, 128), 0)
    routes_copy.wait()
    names_0 = jnp.where(row == routes[0:1, :], 1.0, 0.0)
    names_1 = jnp.where(row == routes[1:2, :], 1.0, 0.0)
    names = names_0 + names_1
    before = jnp.where(row < lane, 1.0, 0.0).astype(BF16)
    position = dot(names.astype(BF16), before)
    position = jnp.where(names > 0.5, position, -1.0)
    slot = row[:CAP].astype(F32)
    places = []
    for e in range(EXPERTS):
        place = jnp.where(slot == position[e : e + 1, :], 1.0, 0.0)
        pmat[e] = place
        places.append(place)
    tok_copy.wait()
    placed = dot(jnp.concatenate(places, axis=0).astype(BF16), tok[...])
    for e in range(EXPERTS):
        rows = placed[CAP * e : CAP * e + CAP]
        for k in range(PARTS):
            left = rows[:, 128 * k : 128 * k + 128]
            right = rows[:, half + 128 * k : half + 128 * k + 128]
            rows_out[k, e] = jnp.concatenate([left, right], axis=0).astype(BF16)

    pl.semaphore_wait(barrier, (EXPERTS - 1) + EXPERTS + 1 + (ZS - 1))

    sends = []
    stores = []

    def finish():
        for copy in sends:
            copy.wait_send()
        for copy in stores:
            copy.wait()

    def remote(src, dst, send_sem, recv_sem, e, d):
        copy = pltpu.make_async_remote_copy(
            src_ref=src,
            dst_ref=dst,
            send_sem=send_sem,
            recv_sem=recv_sem,
            device_id={"expert": e, "etp": d},
            device_id_type=MESH,
        )
        copy.start()
        sends.append(copy)
        return copy

    stage1 = {}
    for k in range(PARTS):
        for o in FAR_FIRST:
            stage1[k, o] = remote(
                rows_out.at[k, peer(o)],
                land.at[0, k, o],
                s1_send.at[k, o],
                s1_recv.at[k, o],
                peer(o),
                near(peer(o)),
            )
    first = [places[e] * names_0[e : e + 1, :] for e in range(EXPERTS)]
    second = [places[e] * names_1[e : e + 1, :] for e in range(EXPERTS)]
    token_of = lax.broadcasted_iota(jnp.int32, (128, 256), 0)
    choice = lax.broadcasted_iota(jnp.int32, (128, 256), 1)
    even = jnp.where(choice == 2 * token_of, 1.0, 0.0).astype(BF16)
    odd = jnp.where(choice == 2 * token_of + 1, 1.0, 0.0).astype(BF16)
    placing = dot(jnp.concatenate(first, axis=0).astype(BF16), even)
    placing = placing + dot(jnp.concatenate(second, axis=0).astype(BF16), odd)
    dh_copy.wait()
    cot = dot(placing.astype(BF16), dh[...])
    for e in range(EXPERTS):
        padded = jnp.concatenate(
            [cot[CAP * e : CAP * e + CAP], jnp.zeros((8, 128), F32)], axis=0
        )
        cot_out[e] = padded.astype(BF16)
    cots = {}
    for o in FAR_FIRST:
        cots[o] = remote(
            cot_out.at[peer(o)], cot_land.at[o], cot_send.at[o], cot_recv.at[o], peer(o), p
        )
    for k in range(PARTS):
        land[0, k, 0] = rows_out[k, expert]
    cot_land[0] = cot_out[expert]
    gather = jnp.concatenate(
        [pmat[peer(o)] for o in range(EXPERTS) for _ in range(2)], axis=0
    ).T.astype(BF16)

    zfwd, c0fwd, c2fwd = {}, {}, {}
    for k in range(PARTS):
        for o in FAR_FIRST:
            stage1[k, o].wait_recv()
        zfwd[k] = remote(land.at[0, k], land.at[2, k], z_send.at[k], z_recv.at[k], expert, z_to)
        c0fwd[k] = remote(
            land.at[0, k], land.at[1, k], c0_send.at[k], c0_recv.at[k], expert, core_mate
        )

    def compact(r, k):
        for j in range(EXPERTS // 2):
            one = land[r, k, 2 * j].astype(F32)
            two = land[r, k, 2 * j + 1].astype(F32)
            left = jnp.concatenate([one[:CAP], two[:CAP]], axis=0)
            right = jnp.concatenate([one[CAP:], two[CAP:]], axis=0)
            at = pl.ds(2 * CAP * j, 2 * CAP)
            srows[r, at, pl.ds(128 * k, 128)] = left.astype(BF16)
            srows[r, at, pl.ds(half + 128 * k, 128)] = right.astype(BF16)

    def forward(r):
        at = pl.multiple_of(quarters[r] * width, 128)
        return dot(srows[r], wcat[pl.ds(at, width), :])

    for k in range(PARTS):
        compact(0, k)
    wg_copy.wait()
    wu_copy.wait()
    acts = forward(0)
    for k in range(PARTS):
        zfwd[k].wait_recv()
        c2fwd[k] = remote(
            land.at[2, k], land.at[3, k], c2_send.at[k], c2_recv.at[k], expert, core_mate
        )
        c0fwd[k].wait_recv()
        compact(1, k)
        compact(2, k)
        if k == PARTS - 2:
            for o in FAR_FIRST:
                cots[o].wait_recv()
            cotangent = jnp.concatenate(
                [cot_land[o].astype(F32)[:CAP] for o in range(EXPERTS)], axis=0
            )
    acts = acts + forward(1)
    acts = acts + forward(2)
    for k in range(PARTS):
        c2fwd[k].wait_recv()
        compact(3, k)
    acts = acts + forward(3)

    gate_act, up_act = acts[:, :BLK], acts[:, BLK:]
    sig = jax.nn.sigmoid(gate_act)
    d_up = cotangent * gate_act * sig
    d_gate = cotangent * up_act * sig * (1.0 + gate_act * (1.0 - sig))
    d_both = jnp.concatenate([d_gate, d_up], axis=1)
    d_rows = d_both.astype(BF16)
    d_both = jnp.concatenate([d_both, jnp.zeros((384 - SLOTS, 2 * BLK), F32)], axis=0)
    d_t = d_both.T.astype(BF16)[:, :SLOTS]

    def grad_piece(r):
        grad = dot(d_t, srows[r])
        hi = grad.astype(BF16)
        lo = (grad - hi.astype(F32)).astype(BF16)
        a_hi[r] = hi
        a_lo[r] = lo
        if r == 0:
            gram[0] = dot_nt(hi, hi)
            gram[1] = dot_nt(hi, lo)
        else:
            gram[0] = gram[0] + dot_nt(hi, hi)
            gram[1] = gram[1] + dot_nt(hi, lo)

    wide_row = lax.broadcasted_iota(jnp.int32, (256, 256), 0)
    wide_lane = lax.broadcasted_iota(jnp.int32, (256, 256), 1)
    state = {}

    def ns_start():
        cross = gram[1]
        g = gram[0] + cross + cross.T
        g = jnp.where((wide_row < BLK) == (wide_lane < BLK), g, 0.0)
        diagonal = jnp.where(wide_row == wide_lane, g, 0.0)
        sum_gate = jnp.sum(diagonal[:BLK], keepdims=True)
        sum_up = jnp.sum(diagonal[BLK:], keepdims=True)
        scale = jnp.where(
            wide_row < BLK, lax.rsqrt(sum_gate + 1e-06), lax.rsqrt(sum_up + 1e-06)
        )
        state["scale"] = scale
        state["g"] = g * scale * scale

    def polynomial(g):
        square = dot_exact(g, g)
        return jnp.where(wide_row == wide_lane, NS_FIRST, 0.0) + NS_SECOND * g + NS_THIRD * square

    def ns_one():
        g = state["g"]
        poly = polynomial(g)
        state["m"] = poly
        state["g"] = dot_exact(dot_exact(g, poly), poly)

    def ns_two():
        g = state["g"]
        poly = polynomial(g)
        both = dot_exact(jnp.concatenate([state["m"], g], axis=0), poly)
        state["m"] = both[:256]
        state["g"] = dot_exact(both[256:], poly)

    def ns_three():
        m = dot_exact(state["m"], polynomial(state["g"])) * state["scale"]
        hi = m.astype(BF16)
        mix[0] = hi
        mix[1] = (m - hi.astype(F32)).astype(BF16)

    def update_piece(r):
        hi = a_hi[r]
        update = dot(mix[0], hi) + dot(mix[1], hi) + dot(mix[0], a_lo[r])
        update = update.T.astype(BF16)
        at = pl.multiple_of(quarters[r] * width, 128)
        for k, out_ref in enumerate((update_gate_ref, update_up_ref)):
            updates[k, r] = update[:, BLK * k : BLK * k + BLK]
            copy = pltpu.make_async_copy(
                updates.at[k, r], out_ref.at[0, pl.ds(at, width)], out_sem.at[k, r]
            )
            copy.start()
            stores.append(copy)

    def back(st, which):
        rows = []
        for side in range(2):
            for dz in ORDER[8 * st : 8 * st + 8]:
                at = ((z + dz) % ZS) * 192 + side * 96 + which * 48
                rows.append(wcat[pl.ds(pl.multiple_of(at, 16), 48), :])
        return dot_nt(d_rows, jnp.concatenate(rows, axis=0))

    tasks = [functools.partial(grad_piece, r) for r in range(4)]
    tasks += [ns_start, ns_one, ns_two, ns_three]
    tasks += [functools.partial(update_piece, r) for r in range(4)]

    def work(count):
        for _ in range(count):
            if tasks:
                tasks.pop(0)()

    swaps = []
    for st in range(2):
        swap_out[st] = back(st, 1 - core).astype(BF16)
        swaps.append(
            remote(
                swap_out.at[st],
                swap_in.at[st],
                swap_send.at[st],
                swap_recv.at[st],
                expert,
                core_mate,
            )
        )
    totals = []
    for st in range(2):
        totals.append(back(st, core))
    for st in range(2):
        swaps[st].wait_recv()
        totals[st] = totals[st] + swap_in[st].astype(F32)

    returns = {}
    for st in range(2):
        out_ref, in_ref = ((first_out, first_in), (later_out, later_in))[st]
        for o in FAR_FIRST + (0,):
            low, high = CAP * o, CAP * o + CAP
            for side in range(2):
                cols = slice(half * side, half * side + half)
                if st == 0:
                    block = jnp.concatenate(
                        [totals[0][low:high, cols], totals[1][high - 8 : high, cols]], axis=0
                    )
                else:
                    block = totals[1][low : high - 8, cols]
                out_ref[o, side] = block.astype(BF16)
            for dy in (1, 0):
                to_y = (y + dy) % 2
                if o == 0 and dy == 0:
                    in_ref[0, 0] = out_ref[0, y]
                    continue
                returns[st, o, dy] = remote(
                    out_ref.at[o, to_y],
                    in_ref.at[o, dy],
                    a2a_send.at[st, o, dy],
                    a2a_recv.at[st, o, dy],
                    back_peer(o),
                    z * 4 + to_y * 2 + core,
                )
    copies = {}
    for st in range(2):
        work(WORK[st])
        got = []
        for o in range(EXPERTS):
            for dy in range(2):
                if (st, o, dy) in returns:
                    returns[st, o, dy].wait_recv()
                first = first_in[o, dy].astype(F32)
                if st == 0:
                    got.append(first[:CAP])
                else:
                    got.append(later_in[o, dy].astype(F32))
                    got.append(first[CAP:])
        part = dot(gather, jnp.concatenate(got, axis=0).astype(BF16)).T
        for i in range(8):
            dz = ORDER[8 * st + i]
            value = part[48 * i : 48 * i + 48]
            if dz == 0:
                mine = value
                continue
            zx_out[dz] = value.astype(BF16)
            copies[dz] = remote(
                zx_out.at[dz],
                zx_in.at[dz],
                zx_send.at[dz],
                zx_recv.at[dz],
                expert,
                (p + 4 * dz) % (4 * ZS),
            )
    work(len(tasks))
    for dz, copy in copies.items():
        copy.wait_recv()
        mine = mine + zx_in[dz].astype(F32)
    d_tokens_ref[...] = mine.astype(BF16)
    finish()


def hand_on(parts, t_ref, a_ref, b_ref, t_out, a_out, b_out, t_held, held, in_sem, out_sem):
    rows = a_ref.shape[1] // parts
    moves = [(t_ref, t_held, t_out, in_sem.at[0, parts], out_sem.at[0, parts])]
    for i in range(parts):
        at = pl.ds(i * rows, rows)
        for k, (src, dst) in enumerate(((a_ref, a_out), (b_ref, b_out))):
            moves.append(
                (src.at[0, at], held.at[k, at], dst.at[0, at], in_sem.at[k, i], out_sem.at[k, i])
            )
    loads = [pltpu.make_async_copy(src, mid, sem) for src, mid, _, sem, _ in moves]
    stores = [pltpu.make_async_copy(mid, dst, sem) for _, mid, dst, _, sem in moves]
    for load in loads:
        load.start()
    for load, store in zip(loads, stores):
        load.wait()
        store.start()
    for store in stores:
        store.wait()


def body(tokens, routes, w_gate, w_up, d_hidden):
    count, model_width = tokens.shape
    units = w_gate.shape[2]
    width = model_width // 4
    half = width // 2
    dma = pltpu.SemaphoreType.DMA
    scratch = [
        pltpu.VMEM((2, count), jnp.int32),
        pltpu.VMEM((count, width), BF16),
        pltpu.VMEM((2 * count, units), BF16),
        pltpu.VMEM((2, 4, width, units), BF16),
        pltpu.VMEM((model_width, 2 * units), BF16),
        pltpu.VMEM((PARTS, EXPERTS, 2 * CAP, 128), BF16),
        pltpu.VMEM((4, PARTS, EXPERTS, 2 * CAP, 128), BF16),
        pltpu.VMEM((EXPERTS, 48, units), BF16),
        pltpu.VMEM((EXPERTS, 48, units), BF16),
        pltpu.VMEM((4, SLOTS, width), BF16),
        pltpu.VMEM((4, 2 * units, width), BF16),
        pltpu.VMEM((4, 2 * units, width), BF16),
        pltpu.VMEM((2, 2 * units, 2 * units), F32),
        pltpu.VMEM((2, 2 * units, 2 * units), BF16),
        pltpu.VMEM((2, SLOTS, width), BF16),
        pltpu.VMEM((2, SLOTS, width), BF16),
        pltpu.VMEM((EXPERTS, 2, CAP + 8, half), BF16),
        pltpu.VMEM((EXPERTS, 2, CAP + 8, half), BF16),
        pltpu.VMEM((EXPERTS, 2, CAP - 8, half), BF16),
        pltpu.VMEM((EXPERTS, 2, CAP - 8, half), BF16),
        pltpu.VMEM((ZS, 48, count), BF16),
        pltpu.VMEM((ZS, 48, count), BF16),
        pltpu.VMEM((EXPERTS, CAP, count), F32),
        dma((5,)),
        dma((2, 4)),
    ]
    for shape in (
        (PARTS, EXPERTS),
        (EXPERTS,),
        (PARTS,),
        (PARTS,),
        (PARTS,),
        (2,),
        (2, EXPERTS, 2),
        (ZS,),
    ):
        scratch += [dma(shape), dma(shape)]
    vmem = pl.BlockSpec(memory_space=pltpu.VMEM)
    anywhere = pl.BlockSpec(memory_space=pl.ANY)
    d_tokens, update_gate, update_up = pl.pallas_call(
        kernel,
        out_shape=(
            jax.ShapeDtypeStruct((48, count), BF16),
            jax.ShapeDtypeStruct(w_gate.shape, BF16),
            jax.ShapeDtypeStruct(w_up.shape, BF16),
        ),
        in_specs=[anywhere] * 5,
        out_specs=(vmem, anywhere, anywhere),
        scratch_shapes=scratch,
        compiler_params=pltpu.CompilerParams(
            collective_id=0, has_side_effects=True, vmem_limit_bytes=56 * 1024 * 1024
        ),
    )(tokens, routes.T, w_gate, w_up, d_hidden.reshape(2 * count, units))
    parts = 4
    d_tokens, update_gate, update_up = pl.pallas_call(
        functools.partial(hand_on, parts),
        out_shape=(
            jax.ShapeDtypeStruct((48, count), BF16),
            jax.ShapeDtypeStruct(w_gate.shape, BF16),
            jax.ShapeDtypeStruct(w_up.shape, BF16),
        ),
        in_specs=[anywhere] * 3,
        out_specs=(anywhere,) * 3,
        scratch_shapes=[
            pltpu.VMEM((48, count), BF16),
            pltpu.VMEM((2, model_width, units), BF16),
            dma((2, parts + 1)),
            dma((2, parts + 1)),
        ],
    )(d_tokens, update_gate, update_up)
    return d_tokens.T, update_gate, update_up


def solution(mesh):
    in_specs = (
        P("expert", None),
        P("expert", None),
        P("expert", None, "etp"),
        P("expert", None, "etp"),
        P("expert", None, "etp"),
    )
    out_specs = (P("expert", "etp"), P("expert", None, "etp"), P("expert", None, "etp"))
    return jax.shard_map(body, mesh=mesh, in_specs=in_specs, out_specs=out_specs, check_vma=False)
```

time: 77.4 us -> 63.6 us (0.82)
  the two profiles are of different devices: /device:TPU:32 before, /device:TPU:1 now
where the time goes in v2:
time: 63.6 us; the launch traced here: 63.5 us
  Pallas kernels  62.8 us (99%)
  between operations  0.64 us (1%)
    pallas_call x1, Pallas kernels, body(): pl.pallas_call(kernel, out_shape=(jax.ShapeDtypeStruct((48, count), BF16)...  60.5 us
    pallas_call x1, Pallas kernels, body(): pl.pallas_call(functools.partial(hand_on, parts), out_shape=(jax.ShapeDty...  2.34 us

profile of v2, /device:TPU:1, one launch (start us, length us, event | category | flops | bytes accessed | tf_op | source)
XLA Modules:
  0.0 63.5 jit_solution(16280164898952488674)
XLA Ops:
  0.6 60.5 %shard_map.76 = (bf16[48,128]{1,0:T(8,128)(2,1)}, bf16[1,3072,128]{2,1,0:T(8,128)(2,1)}, bf16[1,3072,128]{2,1,0:T(8,128)(2,1)}) custom-call(bf16[128,3072]{1,0:T(8,128)(2,1)} %tokens_ref.1, s32[2,128]{1,0:T(2,128)} %bitcast.4, bf16[1,3072,128]{2,1,0:T(8,128)(2,1)} %w_gate_ref.1, bf16[1,3072,128]{2,1,0:T(8,128)(2,1)} %w_up_ref.1, bf16[256,128]{1,0:T(8,128)(2,1)} %bitcast.3), custom_call_target="tpu_custom_call" | custom-call | tf_op jit(solution)/shard_map/pallas_call | solution.py:526
  61.1 2.3 %shard_map.77 = (bf16[48,128]{1,0:T(8,128)(2,1)}, bf16[1,3072,128]{2,1,0:T(8,128)(2,1)}, bf16[1,3072,128]{2,1,0:T(8,128)(2,1)}) custom-call(bf16[48,128]{1,0:T(8,128)(2,1)} %get-tuple-element.9.t_ref, bf16[1,3072,128]{2,1,0:T(8,128)(2,1)} %get-tuple-element.10.a_ref, bf16[1,3072,128]{2,1,0:T(8,128)(2,1)} %get-tuple-element.11.b_ref), custom_call_target="tpu_custom_call" | custom-call | tf_op jit(solution)/shard_map/pallas_call | solution.py:541

commit v3 on v2

--- a/solution.py
+++ b/solution.py
@@ -14,8 +14,11 @@
 SLOTS = EXPERTS * CAP
 PARTS = 3
 FAR_FIRST = (5, 3, 4, 7, 1, 6, 2)
-ORDER = (8, 7, 9, 6, 10, 5, 11, 12, 4, 3, 13, 2, 14, 1, 15, 0)
-WORK = (8, 3, 1)
+GROUPS = ((0, 1, 2, 3), (4, 5, 6, 7))
+ORDER = (8, 7, 9, 6, 10, 5, 11, 4, 12, 3, 13, 2, 14, 1, 15, 0)
+STAGES = 3
+OWNED = 48
+WORK = (8, 2, 1)
 
 NS_FIRST = 3.4445
 NS_SECOND = -4.775
@@ -61,15 +64,21 @@
     a_lo,
     gram,
     mix,
-    swap_out,
-    swap_in,
-    first_out,
-    first_in,
-    later_out,
-    later_in,
+    w_own,
+    w_out,
+    w_in,
+    d_out,
+    d_in,
+    out_0,
+    in_0,
+    out_1,
+    in_1,
+    out_2,
+    in_2,
     zx_out,
     zx_in,
     pmat,
+    known,
     in_sem,
     out_sem,
     s1_send,
@@ -142,7 +151,7 @@
     for o in range(EXPERTS):
         greet(peer(o), y_mate)
     greet(expert, core_mate)
-    for dz in range(1, ZS):
+    for dz in (1, ZS - 1):
         greet(expert, (p + 4 * dz) % (4 * ZS))
 
     lane = lax.broadcasted_iota(jnp.int32, (128, 128), 1)
@@ -169,7 +178,7 @@
             right = rows[:, half + 128 * k : half + 128 * k + 128]
             rows_out[k, e] = jnp.concatenate([left, right], axis=0).astype(BF16)
 
-    pl.semaphore_wait(barrier, (EXPERTS - 1) + EXPERTS + 1 + (ZS - 1))
+    pl.semaphore_wait(barrier, (EXPERTS - 1) + EXPERTS + 1 + 2)
 
     sends = []
     stores = []
@@ -193,9 +202,21 @@
         sends.append(copy)
         return copy
 
+    def tell(step):
+        for dz in (1 << step, ZS - (1 << step)):
+            pl.semaphore_signal(
+                known.at[step],
+                inc=1,
+                device_id={"expert": expert, "etp": (p + 4 * dz) % (4 * ZS)},
+                device_id_type=MESH,
+            )
+
+    def hear(step):
+        pl.semaphore_wait(known.at[step], 2)
+
     stage1 = {}
     for k in range(PARTS):
-        for o in FAR_FIRST:
+        for o in range(1, EXPERTS):
             stage1[k, o] = remote(
                 rows_out.at[k, peer(o)],
                 land.at[0, k, o],
@@ -204,6 +225,7 @@
                 peer(o),
                 near(peer(o)),
             )
+    tell(0)
     first = [places[e] * names_0[e : e + 1, :] for e in range(EXPERTS)]
     second = [places[e] * names_1[e : e + 1, :] for e in range(EXPERTS)]
     token_of = lax.broadcasted_iota(jnp.int32, (128, 256), 0)
@@ -231,15 +253,6 @@
         [pmat[peer(o)] for o in range(EXPERTS) for _ in range(2)], axis=0
     ).T.astype(BF16)
 
-    zfwd, c0fwd, c2fwd = {}, {}, {}
-    for k in range(PARTS):
-        for o in FAR_FIRST:
-            stage1[k, o].wait_recv()
-        zfwd[k] = remote(land.at[0, k], land.at[2, k], z_send.at[k], z_recv.at[k], expert, z_to)
-        c0fwd[k] = remote(
-            land.at[0, k], land.at[1, k], c0_send.at[k], c0_recv.at[k], expert, core_mate
-        )
-
     def compact(r, k):
         for j in range(EXPERTS // 2):
             one = land[r, k, 2 * j].astype(F32)
@@ -250,21 +263,54 @@
             srows[r, at, pl.ds(128 * k, 128)] = left.astype(BF16)
             srows[r, at, pl.ds(half + 128 * k, 128)] = right.astype(BF16)
 
+    zfwd, c0fwd, c2fwd = {}, {}, {}
+
+    def pass_on(copies, k, g, src, dst, send_sem, recv_sem, d):
+        at = pl.ds(GROUPS[g][0], len(GROUPS[g]))
+        copies[k, g] = remote(
+            land.at[src, k, at],
+            land.at[dst, k, at],
+            send_sem.at[k, g],
+            recv_sem.at[k, g],
+            expert,
+            d,
+        )
+
+    for k in range(PARTS):
+        for g, members in enumerate(GROUPS):
+            for o in members:
+                if o > 0:
+                    stage1[k, o].wait_recv()
+            pass_on(zfwd, k, g, 0, 2, z_send, z_recv, z_to)
+            pass_on(c0fwd, k, g, 0, 1, c0_send, c0_recv, core_mate)
+        compact(0, k)
+
     def forward(r):
         at = pl.multiple_of(quarters[r] * width, 128)
         return dot(srows[r], wcat[pl.ds(at, width), :])
 
-    for k in range(PARTS):
-        compact(0, k)
+    def sort_weights(out_ref, which):
+        for side in range(2):
+            for i, dz in enumerate(ORDER):
+                at = ((z + dz) % ZS) * 192 + side * 96 + which * OWNED
+                out_ref[side, pl.ds(OWNED * i, OWNED), :] = wcat[
+                    pl.ds(pl.multiple_of(at, 16), OWNED), :
+                ]
+
     wg_copy.wait()
     wu_copy.wait()
+    sort_weights(w_out, 1 - core)
+    w_swap = remote(w_out, w_in, swap_send.at[0], swap_recv.at[0], expert, core_mate)
+    sort_weights(w_own, core)
+    hear(0)
+    tell(1)
     acts = forward(0)
     for k in range(PARTS):
-        zfwd[k].wait_recv()
-        c2fwd[k] = remote(
-            land.at[2, k], land.at[3, k], c2_send.at[k], c2_recv.at[k], expert, core_mate
-        )
-        c0fwd[k].wait_recv()
+        for g in range(len(GROUPS)):
+            zfwd[k, g].wait_recv()
+            pass_on(c2fwd, k, g, 2, 3, c2_send, c2_recv, core_mate)
+        for g in range(len(GROUPS)):
+            c0fwd[k, g].wait_recv()
         compact(1, k)
         compact(2, k)
         if k == PARTS - 2:
@@ -273,10 +319,13 @@
             cotangent = jnp.concatenate(
                 [cot_land[o].astype(F32)[:CAP] for o in range(EXPERTS)], axis=0
             )
+    hear(1)
+    tell(2)
     acts = acts + forward(1)
     acts = acts + forward(2)
     for k in range(PARTS):
-        c2fwd[k].wait_recv()
+        for g in range(len(GROUPS)):
+            c2fwd[k, g].wait_recv()
         compact(3, k)
     acts = acts + forward(3)
 
@@ -286,6 +335,8 @@
     d_gate = cotangent * up_act * sig * (1.0 + gate_act * (1.0 - sig))
     d_both = jnp.concatenate([d_gate, d_up], axis=1)
     d_rows = d_both.astype(BF16)
+    d_out[...] = d_rows
+    d_swap = remote(d_out, d_in, swap_send.at[1], swap_recv.at[1], expert, core_mate)
     d_both = jnp.concatenate([d_both, jnp.zeros((384 - SLOTS, 2 * BLK), F32)], axis=0)
     d_t = d_both.T.astype(BF16)[:, :SLOTS]
 
@@ -355,14 +406,6 @@
             copy.start()
             stores.append(copy)
 
-    def back(st, which):
-        rows = []
-        for side in range(2):
-            for dz in ORDER[8 * st : 8 * st + 8]:
-                at = ((z + dz) % ZS) * 192 + side * 96 + which * 48
-                rows.append(wcat[pl.ds(pl.multiple_of(at, 16), 48), :])
-        return dot_nt(d_rows, jnp.concatenate(rows, axis=0))
-
     tasks = [functools.partial(grad_piece, r) for r in range(4)]
     tasks += [ns_start, ns_one, ns_two, ns_three]
     tasks += [functools.partial(update_piece, r) for r in range(4)]
@@ -372,40 +415,33 @@
             if tasks:
                 tasks.pop(0)()
 
-    swaps = []
-    for st in range(2):
-        swap_out[st] = back(st, 1 - core).astype(BF16)
-        swaps.append(
-            remote(
-                swap_out.at[st],
-                swap_in.at[st],
-                swap_send.at[st],
-                swap_recv.at[st],
-                expert,
-                core_mate,
-            )
-        )
-    totals = []
-    for st in range(2):
-        totals.append(back(st, core))
-    for st in range(2):
-        swaps[st].wait_recv()
-        totals[st] = totals[st] + swap_in[st].astype(F32)
+    cols = width // STAGES
+
+    def back(rows, weights, st):
+        at = pl.ds(cols * st, cols)
+        return dot_nt(rows, jnp.concatenate([weights[0, at], weights[1, at]], axis=0))
+
+    totals = [back(d_rows, w_own, st) for st in range(STAGES)]
+    w_swap.wait_recv()
+    d_swap.wait_recv()
+    d_mate = d_in[...]
 
     returns = {}
-    for st in range(2):
-        out_ref, in_ref = ((first_out, first_in), (later_out, later_in))[st]
+    for st in range(STAGES):
+        for more in {0: (0, 1), 1: (), 2: (2,)}[st]:
+            totals[more] = totals[more] + back(d_mate, w_in, more)
+        out_ref, in_ref = ((out_0, in_0), (out_1, in_1), (out_2, in_2))[st]
         for o in FAR_FIRST + (0,):
             low, high = CAP * o, CAP * o + CAP
             for side in range(2):
-                cols = slice(half * side, half * side + half)
+                cut = slice(cols * side, cols * side + cols)
                 if st == 0:
-                    block = jnp.concatenate(
-                        [totals[0][low:high, cols], totals[1][high - 8 : high, cols]], axis=0
-                    )
+                    block = [totals[0][low:high, cut], totals[1][high - 8 : high, cut]]
+                elif st == 1:
+                    block = [totals[1][low : high - 8, cut]]
                 else:
-                    block = totals[1][low : high - 8, cols]
-                out_ref[o, side] = block.astype(BF16)
+                    block = [totals[2][low:high, cut], jnp.zeros((8, cols), F32)]
+                out_ref[o, side] = jnp.concatenate(block, axis=0).astype(BF16)
             for dy in (1, 0):
                 to_y = (y + dy) % 2
                 if o == 0 and dy == 0:
@@ -419,28 +455,35 @@
                     back_peer(o),
                     z * 4 + to_y * 2 + core,
                 )
+    hear(2)
     copies = {}
-    for st in range(2):
+    for st in range(STAGES):
         work(WORK[st])
         got = []
         for o in range(EXPERTS):
             for dy in range(2):
                 if (st, o, dy) in returns:
                     returns[st, o, dy].wait_recv()
-                first = first_in[o, dy].astype(F32)
                 if st == 0:
-                    got.append(first[:CAP])
+                    got.append(in_0[o, dy].astype(F32)[:CAP])
+                elif st == 1:
+                    got.append(in_1[o, dy].astype(F32))
+                    got.append(in_0[o, dy].astype(F32)[CAP:])
                 else:
-                    got.append(later_in[o, dy].astype(F32))
-                    got.append(first[CAP:])
+                    got.append(in_2[o, dy].astype(F32)[:CAP])
         part = dot(gather, jnp.concatenate(got, axis=0).astype(BF16)).T
-        for i in range(8):
-            dz = ORDER[8 * st + i]
-            value = part[48 * i : 48 * i + 48]
+        for i, dz in enumerate(ORDER):
+            low = max(OWNED * i, cols * st)
+            high = min(OWNED * i + OWNED, cols * st + cols)
+            if low >= high:
+                continue
+            value = part[low - cols * st : high - cols * st]
             if dz == 0:
                 mine = value
                 continue
-            zx_out[dz] = value.astype(BF16)
+            zx_out[dz, pl.ds(low - OWNED * i, high - low)] = value.astype(BF16)
+            if high < OWNED * i + OWNED:
+                continue
             copies[dz] = remote(
                 zx_out.at[dz],
                 zx_in.at[dz],
@@ -482,6 +525,7 @@
     units = w_gate.shape[2]
     width = model_width // 4
     half = width // 2
+    cols = width // STAGES
     dma = pltpu.SemaphoreType.DMA
     scratch = [
         pltpu.VMEM((2, count), jnp.int32),
@@ -498,26 +542,32 @@
         pltpu.VMEM((4, 2 * units, width), BF16),
         pltpu.VMEM((2, 2 * units, 2 * units), F32),
         pltpu.VMEM((2, 2 * units, 2 * units), BF16),
-        pltpu.VMEM((2, SLOTS, width), BF16),
-        pltpu.VMEM((2, SLOTS, width), BF16),
-        pltpu.VMEM((EXPERTS, 2, CAP + 8, half), BF16),
-        pltpu.VMEM((EXPERTS, 2, CAP + 8, half), BF16),
-        pltpu.VMEM((EXPERTS, 2, CAP - 8, half), BF16),
-        pltpu.VMEM((EXPERTS, 2, CAP - 8, half), BF16),
+        pltpu.VMEM((2, width, 2 * units), BF16),
+        pltpu.VMEM((2, width, 2 * units), BF16),
+        pltpu.VMEM((2, width, 2 * units), BF16),
+        pltpu.VMEM((SLOTS, 2 * units), BF16),
+        pltpu.VMEM((SLOTS, 2 * units), BF16),
+        pltpu.VMEM((EXPERTS, 2, CAP + 8, cols), BF16),
+        pltpu.VMEM((EXPERTS, 2, CAP + 8, cols), BF16),
+        pltpu.VMEM((EXPERTS, 2, CAP - 8, cols), BF16),
+        pltpu.VMEM((EXPERTS, 2, CAP - 8, cols), BF16),
+        pltpu.VMEM((EXPERTS, 2, CAP + 8, cols), BF16),
+        pltpu.VMEM((EXPERTS, 2, CAP + 8, cols), BF16),
         pltpu.VMEM((ZS, 48, count), BF16),
         pltpu.VMEM((ZS, 48, count), BF16),
         pltpu.VMEM((EXPERTS, CAP, count), F32),
+        pltpu.SemaphoreType.REGULAR((3,)),
         dma((5,)),
         dma((2, 4)),
     ]
     for shape in (
         (PARTS, EXPERTS),
         (EXPERTS,),
-        (PARTS,),
-        (PARTS,),
-        (PARTS,),
+        (PARTS, len(GROUPS)),
+        (PARTS, len(GROUPS)),
+        (PARTS, len(GROUPS)),
         (2,),
-        (2, EXPERTS, 2),
+        (STAGES, EXPERTS, 2),
         (ZS,),
     ):
         scratch += [dma(shape), dma(shape)]

time: 63.6 us -> 57.9 us (0.910)
  Pallas kernels: 62.8 us -> 57.1 us
    pallas_call x1, Pallas kernels: 60.5 us -> 54.8 us  [body(): pl.pallas_call(kernel, out_shape=(jax.ShapeDtypeStruct((48, count), BF16)...]
where the time goes in v3:
time: 57.9 us; the launch traced here: 57.8 us
  Pallas kernels  57.1 us (99%)
  between operations  0.64 us (1%)
    pallas_call x1, Pallas kernels, body(): pl.pallas_call(kernel, out_shape=(jax.ShapeDtypeStruct((48, count), BF16)...  54.8 us
    pallas_call x1, Pallas kernels, body(): pl.pallas_call(functools.partial(hand_on, parts), out_shape=(jax.ShapeDty...  2.34 us

profile of v3, /device:TPU:1, one launch (start us, length us, event | category | flops | bytes accessed | tf_op | source)
XLA Modules:
  0.0 57.8 jit_solution(5957641992862050445)
XLA Ops:
  0.6 54.8 %shard_map.76 = (bf16[48,128]{1,0:T(8,128)(2,1)}, bf16[1,3072,128]{2,1,0:T(8,128)(2,1)}, bf16[1,3072,128]{2,1,0:T(8,128)(2,1)}) custom-call(bf16[128,3072]{1,0:T(8,128)(2,1)} %tokens_ref.1, s32[2,128]{1,0:T(2,128)} %bitcast.4, bf16[1,3072,128]{2,1,0:T(8,128)(2,1)} %w_gate_ref.1, bf16[1,3072,128]{2,1,0:T(8,128)(2,1)} %w_up_ref.1, bf16[256,128]{1,0:T(8,128)(2,1)} %bitcast.3), custom_call_target="tpu_custom_call" | custom-call | tf_op jit(solution)/shard_map/pallas_call | solution.py:576
  55.4 2.3 %shard_map.77 = (bf16[48,128]{1,0:T(8,128)(2,1)}, bf16[1,3072,128]{2,1,0:T(8,128)(2,1)}, bf16[1,3072,128]{2,1,0:T(8,128)(2,1)}) custom-call(bf16[48,128]{1,0:T(8,128)(2,1)} %get-tuple-element.9.t_ref, bf16[1,3072,128]{2,1,0:T(8,128)(2,1)} %get-tuple-element.10.a_ref, bf16[1,3072,128]{2,1,0:T(8,128)(2,1)} %get-tuple-element.11.b_ref), custom_call_target="tpu_custom_call" | custom-call | tf_op jit(solution)/shard_map/pallas_call | solution.py:591

commit v4 on v3

--- a/solution.py
+++ b/solution.py
@@ -12,9 +12,8 @@
 BLK = 128
 CAP = 40
 SLOTS = EXPERTS * CAP
-PARTS = 3
 FAR_FIRST = (5, 3, 4, 7, 1, 6, 2)
-GROUPS = ((0, 1, 2, 3), (4, 5, 6, 7))
+PIECES = (256, 512, 512, 256)
 ORDER = (8, 7, 9, 6, 10, 5, 11, 4, 12, 3, 13, 2, 14, 1, 15, 0)
 STAGES = 3
 OWNED = 48
@@ -55,8 +54,13 @@
     dh,
     updates,
     wcat,
-    rows_out,
-    land,
+    rows_out_0,
+    rows_out_1,
+    rows_out_2,
+    land_0,
+    land_1,
+    land_2,
+    land_3,
     cot_out,
     cot_land,
     srows,
@@ -89,8 +93,6 @@
     z_recv,
     c0_send,
     c0_recv,
-    c2_send,
-    c2_recv,
     swap_send,
     swap_recv,
     a2a_send,
@@ -98,13 +100,14 @@
     zx_send,
     zx_recv,
 ):
+    rows_out = (rows_out_0, rows_out_1, rows_out_2)
+    land = (land_0, land_1, land_2, land_3)
     expert = lax.axis_index("expert")
     p = lax.axis_index("etp")
     z = p // 4
     y = (p // 2) % 2
     core = p % 2
-    width = tok.shape[1]
-    half = width // 2
+    width = wcat.shape[0] // 4
 
     def peer(o):
         return (expert + o) % EXPERTS
@@ -113,28 +116,42 @@
         return (expert + EXPERTS - o) % EXPERTS
 
     core_mate = z * 4 + y * 2 + (1 - core)
-    z_to = (p + 4 * ZS + 4 - 8 * core) % (4 * ZS)
     y_mate = z * 4 + (1 - y) * 2 + core
 
     def near(e):
         cross = (expert + e) % 2
         return z * 4 + ((y + cross) % 2) * 2 + core
 
-    own_q = 2 * (z % 2) + core
-    mate_q = 2 * (z % 2) + (1 - core)
-    zown_q = 2 * (1 - z % 2) + core
-    zmate_q = 2 * (1 - z % 2) + (1 - core)
-    quarters = (own_q, mate_q, zown_q, zmate_q)
-
-    tok_copy = pltpu.make_async_copy(
-        tokens_ref.at[:, pl.ds(pl.multiple_of(own_q * width, 128), width)], tok, in_sem.at[0]
-    )
+    z_to = (p + 4 * ZS + 4 - 8 * core) % (4 * ZS)
+
+    def places_of(which):
+        shared = 4 * PIECES[0]
+        kept = shared + which * (PIECES[1] + PIECES[2])
+        return (
+            PIECES[0] * (2 * (z % 2) + which),
+            kept,
+            kept + PIECES[1],
+            PIECES[0] * (2 * (1 - z % 2) + which),
+        )
+
+    starts = (places_of(core), places_of(1 - core))
+
+    lanes = (0, PIECES[0], PIECES[0] + PIECES[1], 2 * width - PIECES[3])
+    tok_copies = [
+        pltpu.make_async_copy(
+            tokens_ref.at[:, pl.ds(pl.multiple_of(starts[0][j], 128), PIECES[j])],
+            tok.at[:, pl.ds(lanes[j], PIECES[j])],
+            in_sem.at[(0, 5, 6)[j]],
+        )
+        for j in range(3)
+    ]
     wg_copy = pltpu.make_async_copy(w_gate_ref.at[0], wcat.at[:, pl.ds(0, BLK)], in_sem.at[1])
     wu_copy = pltpu.make_async_copy(w_up_ref.at[0], wcat.at[:, pl.ds(BLK, BLK)], in_sem.at[2])
     dh_copy = pltpu.make_async_copy(dh_ref, dh, in_sem.at[3])
     routes_copy = pltpu.make_async_copy(routes_ref, routes, in_sem.at[4])
     routes_copy.start()
-    tok_copy.start()
+    for copy in tok_copies:
+        copy.start()
     dh_copy.start()
     wg_copy.start()
     wu_copy.start()
@@ -169,14 +186,15 @@
         place = jnp.where(slot == position[e : e + 1, :], 1.0, 0.0)
         pmat[e] = place
         places.append(place)
-    tok_copy.wait()
+    for copy in tok_copies:
+        copy.wait()
     placed = dot(jnp.concatenate(places, axis=0).astype(BF16), tok[...])
     for e in range(EXPERTS):
         rows = placed[CAP * e : CAP * e + CAP]
-        for k in range(PARTS):
-            left = rows[:, 128 * k : 128 * k + 128]
-            right = rows[:, half + 128 * k : half + 128 * k + 128]
-            rows_out[k, e] = jnp.concatenate([left, right], axis=0).astype(BF16)
+        for j in range(3):
+            mid = lanes[j] + PIECES[j] // 2
+            left, right = rows[:, lanes[j] : mid], rows[:, mid : lanes[j] + PIECES[j]]
+            rows_out[j][e] = jnp.concatenate([left, right], axis=0).astype(BF16)
 
     pl.semaphore_wait(barrier, (EXPERTS - 1) + EXPERTS + 1 + 2)
 
@@ -215,13 +233,13 @@
         pl.semaphore_wait(known.at[step], 2)
 
     stage1 = {}
-    for k in range(PARTS):
+    for j in range(3):
         for o in range(1, EXPERTS):
-            stage1[k, o] = remote(
-                rows_out.at[k, peer(o)],
-                land.at[0, k, o],
-                s1_send.at[k, o],
-                s1_recv.at[k, o],
+            stage1[j, o] = remote(
+                rows_out[j].at[peer(o)],
+                land[j].at[0, o],
+                s1_send.at[j, o],
+                s1_recv.at[j, o],
                 peer(o),
                 near(peer(o)),
             )
@@ -246,48 +264,30 @@
         cots[o] = remote(
             cot_out.at[peer(o)], cot_land.at[o], cot_send.at[o], cot_recv.at[o], peer(o), p
         )
-    for k in range(PARTS):
-        land[0, k, 0] = rows_out[k, expert]
+    for j in range(3):
+        land[j][0, 0] = rows_out[j][expert]
     cot_land[0] = cot_out[expert]
     gather = jnp.concatenate(
         [pmat[peer(o)] for o in range(EXPERTS) for _ in range(2)], axis=0
     ).T.astype(BF16)
 
-    def compact(r, k):
-        for j in range(EXPERTS // 2):
-            one = land[r, k, 2 * j].astype(F32)
-            two = land[r, k, 2 * j + 1].astype(F32)
+    def compact(r, j):
+        mid = PIECES[j] // 2
+        lane_at = lanes[j] % width
+        for i in range(EXPERTS // 2):
+            one = land[j][r, 2 * i].astype(F32)
+            two = land[j][r, 2 * i + 1].astype(F32)
             left = jnp.concatenate([one[:CAP], two[:CAP]], axis=0)
             right = jnp.concatenate([one[CAP:], two[CAP:]], axis=0)
-            at = pl.ds(2 * CAP * j, 2 * CAP)
-            srows[r, at, pl.ds(128 * k, 128)] = left.astype(BF16)
-            srows[r, at, pl.ds(half + 128 * k, 128)] = right.astype(BF16)
-
-    zfwd, c0fwd, c2fwd = {}, {}, {}
-
-    def pass_on(copies, k, g, src, dst, send_sem, recv_sem, d):
-        at = pl.ds(GROUPS[g][0], len(GROUPS[g]))
-        copies[k, g] = remote(
-            land.at[src, k, at],
-            land.at[dst, k, at],
-            send_sem.at[k, g],
-            recv_sem.at[k, g],
-            expert,
-            d,
-        )
-
-    for k in range(PARTS):
-        for g, members in enumerate(GROUPS):
-            for o in members:
-                if o > 0:
-                    stage1[k, o].wait_recv()
-            pass_on(zfwd, k, g, 0, 2, z_send, z_recv, z_to)
-            pass_on(c0fwd, k, g, 0, 1, c0_send, c0_recv, core_mate)
-        compact(0, k)
-
-    def forward(r):
-        at = pl.multiple_of(quarters[r] * width, 128)
-        return dot(srows[r], wcat[pl.ds(at, width), :])
+            at = pl.ds(2 * CAP * i, 2 * CAP)
+            srows[2 * r + j // 2, at, pl.ds(lane_at, mid)] = left.astype(BF16)
+            srows[2 * r + j // 2, at, pl.ds(lane_at + mid, mid)] = right.astype(BF16)
+
+    def forward(r, j):
+        compact(r, j)
+        at = pl.multiple_of(starts[r][j], 128)
+        rows = srows[2 * r + j // 2, :, pl.ds(lanes[j] % width, PIECES[j])]
+        return dot(rows, wcat[pl.ds(at, PIECES[j]), :])
 
     def sort_weights(out_ref, which):
         for side in range(2):
@@ -304,30 +304,45 @@
     sort_weights(w_own, core)
     hear(0)
     tell(1)
-    acts = forward(0)
-    for k in range(PARTS):
-        for g in range(len(GROUPS)):
-            zfwd[k, g].wait_recv()
-            pass_on(c2fwd, k, g, 2, 3, c2_send, c2_recv, core_mate)
-        for g in range(len(GROUPS)):
-            c0fwd[k, g].wait_recv()
-        compact(1, k)
-        compact(2, k)
-        if k == PARTS - 2:
-            for o in FAR_FIRST:
-                cots[o].wait_recv()
-            cotangent = jnp.concatenate(
-                [cot_land[o].astype(F32)[:CAP] for o in range(EXPERTS)], axis=0
+
+    passed = []
+
+    def pass_on(j):
+        passed.append(
+            remote(
+                land[j].at[0], land[j].at[1], c0_send.at[j], c0_recv.at[j], expert, core_mate
             )
+        )
+
+    def arrived(j):
+        for o in range(1, EXPERTS):
+            stage1[j, o].wait_recv()
+
+    arrived(0)
+    along = remote(land[0].at[0], land[3].at[0], z_send.at[0], z_recv.at[0], expert, z_to)
+    pass_on(0)
+    acts = forward(0, 0)
     hear(1)
     tell(2)
-    acts = acts + forward(1)
-    acts = acts + forward(2)
-    for k in range(PARTS):
-        for g in range(len(GROUPS)):
-            c2fwd[k, g].wait_recv()
-        compact(3, k)
-    acts = acts + forward(3)
+    arrived(1)
+    pass_on(1)
+    along.wait_recv()
+    pass_on(3)
+    acts = acts + forward(0, 1)
+    acts = acts + forward(0, 3)
+    passed[0].wait_recv()
+    acts = acts + forward(1, 0)
+    arrived(2)
+    pass_on(2)
+    acts = acts + forward(0, 2)
+    for o in FAR_FIRST:
+        cots[o].wait_recv()
+    cotangent = jnp.concatenate(
+        [cot_land[o].astype(F32)[:CAP] for o in range(EXPERTS)], axis=0
+    )
+    for copy, j in zip(passed[1:], (1, 3, 2)):
+        copy.wait_recv()
+        acts = acts + forward(1, j)
 
     gate_act, up_act = acts[:, :BLK], acts[:, BLK:]
     sig = jax.nn.sigmoid(gate_act)
@@ -397,14 +412,18 @@
         hi = a_hi[r]
         update = dot(mix[0], hi) + dot(mix[1], hi) + dot(mix[0], a_lo[r])
         update = update.T.astype(BF16)
-        at = pl.multiple_of(quarters[r] * width, 128)
-        for k, out_ref in enumerate((update_gate_ref, update_up_ref)):
-            updates[k, r] = update[:, BLK * k : BLK * k + BLK]
-            copy = pltpu.make_async_copy(
-                updates.at[k, r], out_ref.at[0, pl.ds(at, width)], out_sem.at[k, r]
-            )
-            copy.start()
-            stores.append(copy)
+        low = 0
+        for i, j in enumerate((2 * (r % 2), 2 * (r % 2) + 1)):
+            at = pl.ds(pl.multiple_of(starts[r // 2][j], 128), PIECES[j])
+            here = pl.ds(low, PIECES[j])
+            for k, out_ref in enumerate((update_gate_ref, update_up_ref)):
+                updates[k, r, here] = update[low : low + PIECES[j], BLK * k : BLK * k + BLK]
+                copy = pltpu.make_async_copy(
+                    updates.at[k, r, here], out_ref.at[0, at], out_sem.at[k, r, i]
+                )
+                copy.start()
+                stores.append(copy)
+            low += PIECES[j]
 
     tasks = [functools.partial(grad_piece, r) for r in range(4)]
     tasks += [ns_start, ns_one, ns_two, ns_three]
@@ -529,12 +548,12 @@
     dma = pltpu.SemaphoreType.DMA
     scratch = [
         pltpu.VMEM((2, count), jnp.int32),
-        pltpu.VMEM((count, width), BF16),
+        pltpu.VMEM((count, 2 * width - PIECES[3]), BF16),
         pltpu.VMEM((2 * count, units), BF16),
         pltpu.VMEM((2, 4, width, units), BF16),
         pltpu.VMEM((model_width, 2 * units), BF16),
-        pltpu.VMEM((PARTS, EXPERTS, 2 * CAP, 128), BF16),
-        pltpu.VMEM((4, PARTS, EXPERTS, 2 * CAP, 128), BF16),
+        *[pltpu.VMEM((EXPERTS, 2 * CAP, PIECES[j] // 2), BF16) for j in range(3)],
+        *[pltpu.VMEM((2, EXPERTS, 2 * CAP, PIECES[j] // 2), BF16) for j in range(4)],
         pltpu.VMEM((EXPERTS, 48, units), BF16),
         pltpu.VMEM((EXPERTS, 48, units), BF16),
         pltpu.VMEM((4, SLOTS, width), BF16),
@@ -557,15 +576,14 @@
         pltpu.VMEM((ZS, 48, count), BF16),
         pltpu.VMEM((EXPERTS, CAP, count), F32),
         pltpu.SemaphoreType.REGULAR((3,)),
-        dma((5,)),
-        dma((2, 4)),
+        dma((7,)),
+        dma((2, 4, 2)),
     ]
     for shape in (
-        (PARTS, EXPERTS),
+        (3, EXPERTS),
         (EXPERTS,),
-        (PARTS, len(GROUPS)),
-        (PARTS, len(GROUPS)),
-        (PARTS, len(GROUPS)),
+        (1,),
+        (4,),
         (2,),
         (STAGES, EXPERTS, 2),
         (ZS,),

time: 57.9 us -> 56.4 us (0.974)
  Pallas kernels: 57.1 us -> 55.6 us
    pallas_call x1, Pallas kernels: 54.8 us -> 53.3 us  [body(): pl.pallas_call(kernel, out_shape=(jax.ShapeDtypeStruct((48, count), BF16)...]
where the time goes in v4:
time: 56.4 us; the launch traced here: 56.3 us
  Pallas kernels  55.6 us (99%)
  between operations  0.64 us (1%)
    pallas_call x1, Pallas kernels, body(): pl.pallas_call(kernel, out_shape=(jax.ShapeDtypeStruct((48, count), BF16)...  53.3 us
    pallas_call x1, Pallas kernels, body(): pl.pallas_call(functools.partial(hand_on, parts), out_shape=(jax.ShapeDty...  2.34 us

profile of v4, /device:TPU:1, one launch (start us, length us, event | category | flops | bytes accessed | tf_op | source)
XLA Modules:
  0.0 56.3 jit_solution(5531182532249290240)
XLA Ops:
  0.6 53.3 %shard_map.76 = (bf16[48,128]{1,0:T(8,128)(2,1)}, bf16[1,3072,128]{2,1,0:T(8,128)(2,1)}, bf16[1,3072,128]{2,1,0:T(8,128)(2,1)}) custom-call(bf16[128,3072]{1,0:T(8,128)(2,1)} %tokens_ref.1, s32[2,128]{1,0:T(2,128)} %bitcast.4, bf16[1,3072,128]{2,1,0:T(8,128)(2,1)} %w_gate_ref.1, bf16[1,3072,128]{2,1,0:T(8,128)(2,1)} %w_up_ref.1, bf16[256,128]{1,0:T(8,128)(2,1)} %bitcast.3), custom_call_target="tpu_custom_call" | custom-call | tf_op jit(solution)/shard_map/pallas_call | solution.py:594
  53.9 2.3 %shard_map.77 = (bf16[48,128]{1,0:T(8,128)(2,1)}, bf16[1,3072,128]{2,1,0:T(8,128)(2,1)}, bf16[1,3072,128]{2,1,0:T(8,128)(2,1)}) custom-call(bf16[48,128]{1,0:T(8,128)(2,1)} %get-tuple-element.9.t_ref, bf16[1,3072,128]{2,1,0:T(8,128)(2,1)} %get-tuple-element.10.a_ref, bf16[1,3072,128]{2,1,0:T(8,128)(2,1)} %get-tuple-element.11.b_ref), custom_call_target="tpu_custom_call" | custom-call | tf_op jit(solution)/shard_map/pallas_call | solution.py:609

commit v5 on v4

--- a/solution.py
+++ b/solution.py
@@ -73,12 +73,8 @@
     w_in,
     d_out,
     d_in,
-    out_0,
-    in_0,
-    out_1,
-    in_1,
-    out_2,
-    in_2,
+    sums_out,
+    sums_in,
     zx_out,
     zx_in,
     pmat,
@@ -447,19 +443,15 @@
 
     returns = {}
     for st in range(STAGES):
-        for more in {0: (0, 1), 1: (), 2: (2,)}[st]:
-            totals[more] = totals[more] + back(d_mate, w_in, more)
-        out_ref, in_ref = ((out_0, in_0), (out_1, in_1), (out_2, in_2))[st]
+        totals[st] = totals[st] + back(d_mate, w_in, st)
+        out_ref, in_ref = sums_out.at[st], sums_in.at[st]
         for o in FAR_FIRST + (0,):
             low, high = CAP * o, CAP * o + CAP
             for side in range(2):
-                cut = slice(cols * side, cols * side + cols)
-                if st == 0:
-                    block = [totals[0][low:high, cut], totals[1][high - 8 : high, cut]]
-                elif st == 1:
-                    block = [totals[1][low : high - 8, cut]]
-                else:
-                    block = [totals[2][low:high, cut], jnp.zeros((8, cols), F32)]
+                block = [
+                    totals[st][low:high, at : at + cols // 2]
+                    for at in (cols * side, cols * side + cols // 2)
+                ]
                 out_ref[o, side] = jnp.concatenate(block, axis=0).astype(BF16)
             for dy in (1, 0):
                 to_y = (y + dy) % 2
@@ -478,19 +470,16 @@
     copies = {}
     for st in range(STAGES):
         work(WORK[st])
-        got = []
+        left, right = [], []
         for o in range(EXPERTS):
             for dy in range(2):
                 if (st, o, dy) in returns:
                     returns[st, o, dy].wait_recv()
-                if st == 0:
-                    got.append(in_0[o, dy].astype(F32)[:CAP])
-                elif st == 1:
-                    got.append(in_1[o, dy].astype(F32))
-                    got.append(in_0[o, dy].astype(F32)[CAP:])
-                else:
-                    got.append(in_2[o, dy].astype(F32)[:CAP])
-        part = dot(gather, jnp.concatenate(got, axis=0).astype(BF16)).T
+                block = sums_in[st, o, dy].astype(F32)
+                left.append(block[:CAP])
+                right.append(block[CAP:])
+        got = [jnp.concatenate(left, axis=0), jnp.concatenate(right, axis=0)]
+        part = dot(gather, jnp.concatenate(got, axis=1).astype(BF16)).T
         for i, dz in enumerate(ORDER):
             low = max(OWNED * i, cols * st)
             high = min(OWNED * i + OWNED, cols * st + cols)
@@ -566,12 +555,8 @@
         pltpu.VMEM((2, width, 2 * units), BF16),
         pltpu.VMEM((SLOTS, 2 * units), BF16),
         pltpu.VMEM((SLOTS, 2 * units), BF16),
-        pltpu.VMEM((EXPERTS, 2, CAP + 8, cols), BF16),
-        pltpu.VMEM((EXPERTS, 2, CAP + 8, cols), BF16),
-        pltpu.VMEM((EXPERTS, 2, CAP - 8, cols), BF16),
-        pltpu.VMEM((EXPERTS, 2, CAP - 8, cols), BF16),
-        pltpu.VMEM((EXPERTS, 2, CAP + 8, cols), BF16),
-        pltpu.VMEM((EXPERTS, 2, CAP + 8, cols), BF16),
+        pltpu.VMEM((STAGES, EXPERTS, 2, 2 * CAP, cols // 2), BF16),
+        pltpu.VMEM((STAGES, EXPERTS, 2, 2 * CAP, cols // 2), BF16),
         pltpu.VMEM((ZS, 48, count), BF16),
         pltpu.VMEM((ZS, 48, count), BF16),
         pltpu.VMEM((EXPERTS, CAP, count), F32),

time: 56.4 us -> 56.3 us (level)
  no operation moved by 1% of the time
where the time goes in v5:
time: 56.3 us; the launch traced here: 55.8 us
  Pallas kernels  55.2 us (98%)
  between operations  0.64 us (1%)
    pallas_call x1, Pallas kernels, body(): pl.pallas_call(kernel, out_shape=(jax.ShapeDtypeStruct((48, count), BF16)...  52.8 us
    pallas_call x1, Pallas kernels, body(): pl.pallas_call(functools.partial(hand_on, parts), out_shape=(jax.ShapeDty...  2.34 us

profile of v5, /device:TPU:1, one launch (start us, length us, event | category | flops | bytes accessed | tf_op | source)
XLA Modules:
  0.0 55.8 jit_solution(1347793960586569703)
XLA Ops:
  0.6 52.8 %shard_map.76 = (bf16[48,128]{1,0:T(8,128)(2,1)}, bf16[1,3072,128]{2,1,0:T(8,128)(2,1)}, bf16[1,3072,128]{2,1,0:T(8,128)(2,1)}) custom-call(bf16[128,3072]{1,0:T(8,128)(2,1)} %tokens_ref.1, s32[2,128]{1,0:T(2,128)} %bitcast.4, bf16[1,3072,128]{2,1,0:T(8,128)(2,1)} %w_gate_ref.1, bf16[1,3072,128]{2,1,0:T(8,128)(2,1)} %w_up_ref.1, bf16[256,128]{1,0:T(8,128)(2,1)} %bitcast.3), custom_call_target="tpu_custom_call" | custom-call | tf_op jit(solution)/shard_map/pallas_call | solution.py:579
  53.5 2.3 %shard_map.77 = (bf16[48,128]{1,0:T(8,128)(2,1)}, bf16[1,3072,128]{2,1,0:T(8,128)(2,1)}, bf16[1,3072,128]{2,1,0:T(8,128)(2,1)}) custom-call(bf16[48,128]{1,0:T(8,128)(2,1)} %get-tuple-element.9.t_ref, bf16[1,3072,128]{2,1,0:T(8,128)(2,1)} %get-tuple-element.10.a_ref, bf16[1,3072,128]{2,1,0:T(8,128)(2,1)} %get-tuple-element.11.b_ref), custom_call_target="tpu_custom_call" | custom-call | tf_op jit(solution)/shard_map/pallas_call | solution.py:594

commit v6 on v5

--- a/solution.py
+++ b/solution.py
@@ -182,18 +182,6 @@
         place = jnp.where(slot == position[e : e + 1, :], 1.0, 0.0)
         pmat[e] = place
         places.append(place)
-    for copy in tok_copies:
-        copy.wait()
-    placed = dot(jnp.concatenate(places, axis=0).astype(BF16), tok[...])
-    for e in range(EXPERTS):
-        rows = placed[CAP * e : CAP * e + CAP]
-        for j in range(3):
-            mid = lanes[j] + PIECES[j] // 2
-            left, right = rows[:, lanes[j] : mid], rows[:, mid : lanes[j] + PIECES[j]]
-            rows_out[j][e] = jnp.concatenate([left, right], axis=0).astype(BF16)
-
-    pl.semaphore_wait(barrier, (EXPERTS - 1) + EXPERTS + 1 + 2)
-
     sends = []
     stores = []
 
@@ -229,7 +217,17 @@
         pl.semaphore_wait(known.at[step], 2)
 
     stage1 = {}
+    by_slot = jnp.concatenate(places, axis=0).astype(BF16)
     for j in range(3):
+        tok_copies[j].wait()
+        placed = dot(by_slot, tok[:, lanes[j] : lanes[j] + PIECES[j]])
+        mid = PIECES[j] // 2
+        for e in range(EXPERTS):
+            rows = placed[CAP * e : CAP * e + CAP]
+            rows = jnp.concatenate([rows[:, :mid], rows[:, mid:]], axis=0)
+            rows_out[j][e] = rows.astype(BF16)
+        if j == 0:
+            pl.semaphore_wait(barrier, (EXPERTS - 1) + EXPERTS + 1 + 2)
         for o in range(1, EXPERTS):
             stage1[j, o] = remote(
                 rows_out[j].at[peer(o)],

time: 56.3 us -> 56.5 us (level)
  no operation moved by 1% of the time
where the time goes in v6:
time: 56.5 us; the launch traced here: 55.8 us
  Pallas kernels  55.2 us (98%)
  between operations  0.64 us (1%)
    pallas_call x1, Pallas kernels, body(): pl.pallas_call(kernel, out_shape=(jax.ShapeDtypeStruct((48, count), BF16)...  52.8 us
    pallas_call x1, Pallas kernels, body(): pl.pallas_call(functools.partial(hand_on, parts), out_shape=(jax.ShapeDty...  2.34 us

profile of v6, /device:TPU:1, one launch (start us, length us, event | category | flops | bytes accessed | tf_op | source)
XLA Modules:
  0.0 55.8 jit_solution(649437738397691312)
XLA Ops:
  0.6 52.8 %shard_map.76 = (bf16[48,128]{1,0:T(8,128)(2,1)}, bf16[1,3072,128]{2,1,0:T(8,128)(2,1)}, bf16[1,3072,128]{2,1,0:T(8,128)(2,1)}) custom-call(bf16[128,3072]{1,0:T(8,128)(2,1)} %tokens_ref.1, s32[2,128]{1,0:T(2,128)} %bitcast.4, bf16[1,3072,128]{2,1,0:T(8,128)(2,1)} %w_gate_ref.1, bf16[1,3072,128]{2,1,0:T(8,128)(2,1)} %w_up_ref.1, bf16[256,128]{1,0:T(8,128)(2,1)} %bitcast.3), custom_call_target="tpu_custom_call" | custom-call | tf_op jit(solution)/shard_map/pallas_call | solution.py:577
  53.5 2.3 %shard_map.77 = (bf16[48,128]{1,0:T(8,128)(2,1)}, bf16[1,3072,128]{2,1,0:T(8,128)(2,1)}, bf16[1,3072,128]{2,1,0:T(8,128)(2,1)}) custom-call(bf16[48,128]{1,0:T(8,128)(2,1)} %get-tuple-element.9.t_ref, bf16[1,3072,128]{2,1,0:T(8,128)(2,1)} %get-tuple-element.10.a_ref, bf16[1,3072,128]{2,1,0:T(8,128)(2,1)} %get-tuple-element.11.b_ref), custom_call_target="tpu_custom_call" | custom-call | tf_op jit(solution)/shard_map/pallas_call | solution.py:592
